TPU v7x, 1024 devices: a whole 4x8x16 slice. The times are simulated.
1024 devices in a mesh: gx: 32 (over y, x), gy: 4 (over z_hi), gz: 8 (over z_lo, core).
Axes of the slice: x: 4, y: 8, z: 16 (z_hi: 4, z_lo: 4; z = z_hi * 4 + z_lo), core: 2. Of those that a mesh axis runs over, the one named last changes fastest.
Arguments:
- amplitudes: float32 [5, 256, 12288], P(None, 'gz', ('gx', 'gy')), may hold values from -24 to 24
- integrals: float32 [5, 12288, 12288], P(None, 'gx', ('gy', 'gz')), may hold values from -0.0546875 to 0.0546875
- pair_counts: int32 [5], replicated, may hold values from 1 to 12288, 57600 in all
- row_counts: int32 [5], replicated, may hold values from 1 to 256, 1000 in all
Outputs:
- cycle_residual: float32 [5, 256, 12288], P(None, 'gx', ('gy', 'gz'))
Inputs may be any that keep to these rules, and one draw needn't show every extreme that they name: `pair_counts`: used pair slots of each block; they sum to 57600 and some block uses all 12288. `row_counts`: used row slots of each block; they sum to 1000 and some block uses all 256.
All inputs are finite; a program needn't handle non-finite values.
Results may differ from a plain program's by a relative error of at most 0.0003.
Values sent between devices are 32-bit elements; how exact they have to be, the bound alone decides.
No kernel may reach another device: no remote copies, remote signals or barrier semaphores. Data moves between devices by JAX's collectives and lax.ppermute only.
A program may use at most 32 MiB of HBM per device.

v0:
```python
import jax
import jax.numpy as jnp
from jax import lax
from jax.sharding import PartitionSpec as P


def contract(left, right):
    return jnp.einsum(
        "brk,bkn->brn",
        left,
        right,
        precision=lax.Precision.HIGHEST,
        preferred_element_type=jnp.float32,
    )


def per_device(amplitudes, integrals, pair_counts, row_counts):
    blocks = amplitudes.shape[0]
    row_local = amplitudes.shape[1]
    pair_local = amplitudes.shape[2]
    column_local = integrals.shape[2]
    row_first = lax.axis_index("gz") * row_local
    pair_first = (lax.axis_index("gx") * lax.axis_size("gy") + lax.axis_index("gy")) * pair_local
    row_ids = row_first + lax.iota(jnp.int32, row_local)
    pair_ids = pair_first + lax.iota(jnp.int32, pair_local)
    row_used = row_ids[None, :] < row_counts[:, None]
    pair_used = pair_ids[None, :] < pair_counts[:, None]
    keep = jnp.logical_and(row_used[:, :, None], pair_used[:, None, :])
    masked = jnp.where(keep, amplitudes, jnp.zeros_like(amplitudes))
    partial_sum = None
    stacked = lax.all_gather(masked[None], ("gy", "gz"), axis=0, tiled=True)
    count_gy = lax.axis_size("gy")
    count_gz = lax.axis_size("gz")
    stacked = stacked.reshape(count_gy, count_gz, blocks, row_local, pair_local)
    slab = jnp.transpose(stacked, (2, 1, 3, 0, 4)).reshape(
        blocks, count_gz * row_local, count_gy * pair_local
    )
    partial_sum = contract(slab, integrals)
    reduced = lax.psum_scatter(partial_sum, "gx", scatter_dimension=1, tiled=True)
    column_first = (
        lax.axis_index("gy") * lax.axis_size("gz") + lax.axis_index("gz")
    ) * column_local
    column_ids = column_first + lax.iota(jnp.int32, column_local)
    column_used = column_ids[None, :] < pair_counts[:, None]
    return jnp.where(column_used[:, None, :], reduced, jnp.zeros_like(reduced))


def solution(mesh):
    placed = (P(None, "gz", ("gx", "gy")), P(None, "gx", ("gy", "gz")), P(), P())
    return jax.shard_map(
        per_device,
        mesh=mesh,
        in_specs=placed,
        out_specs=P(None, "gx", ("gy", "gz")),
        check_vma=False,
    )
```

profile of v0, /device:TPU:1, one launch (start us, length us, event | category | flops | bytes accessed | tf_op | source)
XLA Modules:
  0.0 331.3 jit_solution(3409062845368031513)
XLA Ops:
  6.5 0.0 copy-start
  6.5 0.0 all-gather.3.cloned.1.call-start
  6.5 0.9 broadcast_compare_fusion.1
  7.4 0.7 broadcast_compare_fusion.2
  8.2 1.6 and_select_fusion
  9.8 0.0 all-gather.3.cloned.1.call-update
  9.8 0.0 reduce-scatter.2.cloned.1.call-start
  9.8 85.5 %all-gather.3.cloned.1.call-done = f32[160,32,96]{2,1,0:T(8,128)} async-done(((f32[5,32,96]{2,1,0:T(8,128)}), f32[160,32,96]{2,1,0:T(8,128)}) %all-gather.3.cloned.1.call-update) | async-done | bytes 1966096 | tf_op jit(solution)/shard_map/all_gather | solution.py:31
  95.4 5.6 %copy.8 = f32[4,8,5,32,96]{4,0,3,1,2:T(4,128)} copy(f32[4,8,5,32,96]{4,3,2,1,0:T(8,128)} %bitcast.7) | data formatting | bytes 3932160 | tf_op jit(solution)/shard_map/reshape | solution.py:34
  100.9 3.9 %reshape.91 = f32[5,256,384]{2,1,0:T(8,128)} reshape(f32[5,8,32,4,96]{4,3,2,1,0:T(4,128)} %bitcast.6) | data formatting | bytes 3932160 | tf_op jit(solution)/shard_map/reshape | solution.py:35
  104.8 0.0 copy-done
  104.8 0.0 copy-start.1
  104.8 6.7 %fusion = f32[5,256,384]{2,1,0:T(8,128)} fusion(f32[5,256,384]{2,1,0:T(8,128)} %reshape.91, f32[5,384,384]{2,1,0:T(8,128)S(1)} %copy-done), kind=kOutput, calls=%fused_computation.9 | convolution fusion | flops 2264924160 | bytes 6881280 | tf_op jit(solution)/shard_map/brk,bkn->brn/dot_general | solution.py:8
  111.5 0.0 reduce-scatter.2.cloned.1.call-update
  111.6 0.0 copy-done.1
  111.6 0.1 broadcast_compare_fusion
  111.7 211.4 %reduce-scatter.2.cloned.1.call-done = f32[5,8,384]{2,1,0:T(8,128)} async-done(((f32[5,256,384]{2,1,0:T(8,128)}), f32[5,8,384]{2,1,0:T(8,128)}) %reduce-scatter.2.cloned.1.call-update) | async-done | bytes 61456 | tf_op jit(solution)/shard_map/reduce_scatter | solution.py:39
  323.0 1.5 broadcast_select_fusion
  (3 shorter events, 0.0 us)
Async XLA Ops:
  6.5 98.2 %copy-start = (f32[5,384,384]{2,1,0:T(8,128)S(1)}, f32[5,384,384]{2,1,0:T(8,128)}, u32[]{:S(2)}) copy-start(f32[5,384,384]{2,1,0:T(8,128)} %param.5) | copy-start | bytes 8847364
  6.5 88.8 %all-gather.3.cloned.1.call-start = ((), (), s32[]{:S(2)}) async-start(), calls=%async_computation.2 | async-start | bytes 2703360 | tf_op jit(solution)/shard_map/all_gather | solution.py:31
  9.8 313.2 %reduce-scatter.2.cloned.1.call-start = ((), (), s32[]{:S(2)}) async-start(), calls=%async_computation.1 | async-start | bytes 2027520 | tf_op jit(solution)/shard_map/reduce_scatter | solution.py:39
  104.8 6.8 %copy-start.1 = (s32[5]{0:T(128)S(1)}, s32[5]{0:T(128)}, u32[]{:S(2)}) copy-start(s32[5]{0:T(128)} %param.6) | copy-start | bytes 64
Sparse Core Ops, SparseCore 0:
  10.1 85.2 all-gather.2
  111.7 211.2 reduce-scatter.1
where the time goes:
time: 336 us; the launch traced here: 331 us
  waiting for transfers between devices  297 us (88%)
  between operations  13.4 us (4%)
  local copies, waits for them, and re-layouts  9.43 us (3%)
  matrix products  6.75 us (2%)
  other arithmetic  4.77 us (1%)
    reduce_scatter x1, waiting for transfers between devices, per_device(): lax.psum_scatter(partial_sum, 'gx', scatter_dimension=1, tiled=True)  211 us
    all_gather x1, waiting for transfers between devices, per_device(): stacked = lax.all_gather(masked[None], ('gy', 'gz'), axis=0, tiled=True)  85.5 us
    dot_general x1, matrix products, contract(): jnp.einsum('brk,bkn->brn', left, right, precision=lax.Precision.HIGHEST,...  6.75 us
  transfers between devices with their start and end apart: 2, of which 2 were waited for; matrix products, arithmetic and copies ran while one was open for 0% of the time, Pallas kernels for 0%

commit v1 on v0

v1 whole, which is shorter than its diff:
```python
import functools

import jax
import jax.numpy as jnp
from jax import lax
from jax.experimental import pallas as pl
from jax.experimental.pallas import tpu as pltpu
from jax.sharding import Mesh
from jax.sharding import PartitionSpec as P

NX, NY, ZH, ZL, CORES = 4, 8, 4, 4, 2
BLOCKS, ROWS, PAIRS, COLS = 5, 32, 96, 384
LANES = 128


def product(counts_ref, where_ref, own_ref, other_ref, integrals_ref, out_ref, ahi, alo, bhi, blo):
    g = pl.program_id(0)

    @pl.when(g == 0)
    def _():
        for ref in (ahi, alo, bhi, blo):
            ref[...] = jnp.zeros_like(ref)

    core = where_ref[0]
    left = counts_ref[g] - where_ref[1]
    half = ZL * ROWS
    lane = lax.broadcasted_iota(jnp.int32, (half, PAIRS), 1)
    for h in range(ZH):
        keep = lane + h * PAIRS < left
        for part, ref in enumerate((own_ref, other_ref)):
            a = ref[h * ZL:(h + 1) * ZL, 0].reshape(half, PAIRS)
            a = jnp.where(keep, a, 0.0)
            high = a.astype(jnp.bfloat16)
            low = (a - high.astype(jnp.float32)).astype(jnp.bfloat16)
            ahi[part * half:(part + 1) * half, h * LANES:h * LANES + PAIRS] = high
            alo[part * half:(part + 1) * half, h * LANES:h * LANES + PAIRS] = low
        b = integrals_ref[0, h * PAIRS:(h + 1) * PAIRS, :]
        high = b.astype(jnp.bfloat16)
        bhi[h * LANES:h * LANES + PAIRS, :] = high
        blo[h * LANES:h * LANES + PAIRS, :] = (b - high.astype(jnp.float32)).astype(jnp.bfloat16)
    dot = functools.partial(jnp.dot, preferred_element_type=jnp.float32)
    total = dot(ahi[...], bhi[...]) + (dot(ahi[...], blo[...]) + dot(alo[...], bhi[...]))
    for part in range(CORES):
        side = core if part == 0 else 1 - core
        for l in range(ZL):
            for x in range(NX):
                first = part * half + l * ROWS + x * 8
                out_ref[x, 2 * l + side, 0] = total[first:first + 8]


def per_device(amplitudes, integrals, pair_counts, row_counts):
    gx = lax.axis_index("y") * NX + lax.axis_index("x")
    core = lax.axis_index("c")
    own = lax.all_gather(amplitudes, ("zh", "zl"), axis=0, tiled=False)
    other = lax.ppermute(own, "c", [(0, 1), (1, 0)])
    where = jnp.stack([core, gx * COLS]).astype(jnp.int32)
    slab = pl.BlockSpec((ZH * ZL, 1, ROWS, PAIRS), lambda g, *_: (0, g, 0, 0))
    partial = pl.pallas_call(
        product,
        out_shape=jax.ShapeDtypeStruct((NX, NY, BLOCKS, 8, COLS), jnp.float32),
        grid_spec=pltpu.PrefetchScalarGridSpec(
            num_scalar_prefetch=2,
            grid=(BLOCKS,),
            in_specs=[slab, slab, pl.BlockSpec((1, COLS, COLS), lambda g, *_: (g, 0, 0))],
            out_specs=pl.BlockSpec((NX, NY, 1, 8, COLS), lambda g, *_: (0, 0, g, 0, 0)),
            scratch_shapes=[pltpu.VMEM((CORES * ZL * ROWS, ZH * LANES), jnp.bfloat16)] * 2
            + [pltpu.VMEM((ZH * LANES, COLS), jnp.bfloat16)] * 2,
        ),
        compiler_params=pltpu.CompilerParams(vmem_limit_bytes=24 * 1024 * 1024),
        cost_estimate=pl.CostEstimate(flops=1_200_000_000, bytes_accessed=8_000_000, transcendentals=0),
    )(pair_counts, where, own, other, integrals)
    along_x = lax.all_to_all(partial, "x", 0, 0, tiled=True).sum(0)
    along_y = lax.all_to_all(along_x, "y", 0, 0, tiled=True).sum(0)
    column_first = (lax.axis_index("zh") * ZL * CORES + lax.axis_index("zl") * CORES + core) * COLS
    column_used = column_first + lax.iota(jnp.int32, COLS)[None, :] < pair_counts[:, None]
    row_used = gx * 8 + lax.iota(jnp.int32, 8)[None, :] < row_counts[:, None]
    keep = jnp.logical_and(row_used[:, :, None], column_used[:, None, :])
    return jnp.where(keep, along_y, 0.0)


def solution(mesh):
    fine = Mesh(mesh.devices.reshape(NY, NX, ZH, ZL, CORES), ("y", "x", "zh", "zl", "c"))
    out = P(None, ("y", "x"), ("zh", "zl", "c"))
    return jax.shard_map(
        per_device,
        mesh=fine,
        in_specs=(P(None, ("zl", "c"), ("y", "x", "zh")), out, P(), P()),
        out_specs=out,
        check_vma=False,
    )
```

time: 336 us -> 115 us (0.34); the launches traced: 331 us -> 114 us
  waiting for transfers between devices: 297 us -> 17.1 us
  blocking collectives: 0 us -> 72.1 us
  starting transfers between devices: 0.04 us -> 16.6 us
  between operations: 13.4 us -> 0.05 us
  local copies, waits for them, and re-layouts: 9.43 us -> 2.49 us
  matrix products: 6.75 us -> 0 us
  Pallas kernels: 0 us -> 4.17 us
    reduce_scatter x1 -> x0, waiting for transfers between devices: 211 us -> none  [per_device(): lax.psum_scatter(partial_sum, 'gx', scatter_dimension=1, tiled=True)]
    all_gather x1 -> x0, waiting for transfers between devices: 85.5 us -> none  [per_device(): stacked = lax.all_gather(masked[None], ('gy', 'gz'), axis=0, tiled=True)]
    all_gather x0 -> x1, blocking collectives: none -> 44.2 us  [per_device(): own = lax.all_gather(amplitudes, ('zh', 'zl'), axis=0, tiled=False)]
    all_to_all x0 -> x1, blocking collectives: none -> 27.9 us  [per_device(): along_x = lax.all_to_all(partial, 'x', 0, 0, tiled=True).sum(0)]
    all_to_all x0 -> x1, waiting for transfers between devices: none -> 14.5 us  [per_device(): along_y = lax.all_to_all(along_x, 'y', 0, 0, tiled=True).sum(0)]
    ppermute x0 -> x1, starting transfers between devices: none -> 9.74 us  [per_device(): other = lax.ppermute(own, 'c', [(0, 1), (1, 0)])]
    reshape x2 -> x0, local copies, waits for them, and re-layouts: 9.42 us -> none  [the longest x1 5.56 us: per_device(): stacked = stacked.reshape(count_gy, count_gz, blocks, row_local, pair_local)]
    all_to_all x0 -> x1, starting transfers between devices: none -> 6.83 us  [per_device(): along_y = lax.all_to_all(along_x, 'y', 0, 0, tiled=True).sum(0)]
where the time goes in v1:
time: 115 us; the launch traced here: 114 us
  blocking collectives  72.1 us (63%)
  waiting for transfers between devices  17.1 us (15%)
  starting transfers between devices  16.6 us (14%)
  Pallas kernels  4.17 us (4%)
  local copies, waits for them, and re-layouts  2.49 us (2%)
  other arithmetic  1.88 us (2%)
    all_gather x1, blocking collectives, per_device(): own = lax.all_gather(amplitudes, ('zh', 'zl'), axis=0, tiled=False)  44.2 us
    all_to_all x1, blocking collectives, per_device(): along_x = lax.all_to_all(partial, 'x', 0, 0, tiled=True).sum(0)  27.9 us
    all_to_all x1, waiting for transfers between devices, per_device(): along_y = lax.all_to_all(along_x, 'y', 0, 0, tiled=True).sum(0)  14.5 us
    ppermute x1, starting transfers between devices, per_device(): other = lax.ppermute(own, 'c', [(0, 1), (1, 0)])  9.74 us
    all_to_all x1, starting transfers between devices, per_device(): along_y = lax.all_to_all(along_x, 'y', 0, 0, tiled=True).sum(0)  6.83 us
    pallas_call x1, Pallas kernels, per_device(): pl.pallas_call(product, out_shape=jax.ShapeDtypeStruct((NX, NY, BLOCKS, 8...  4.17 us
    ppermute x1, waiting for transfers between devices, per_device(): other = lax.ppermute(own, 'c', [(0, 1), (1, 0)])  2.56 us
    unnamed x8, local copies, waits for them, and re-layouts  2.49 us
  transfers between devices with their start and end apart: 2, of which 2 were waited for; matrix products, arithmetic and copies ran while one was open for 0% of the time, Pallas kernels for 0%

profile of v1, /device:TPU:1, one launch (start us, length us, event | category | flops | bytes accessed | tf_op | source)
XLA Modules:
  0.0 114.4 jit_solution(15062008242820778424)
XLA Ops:
  0.0 44.2 %all-gather = f32[80,32,96]{2,1,0:T(8,128)S(1)} all-gather(f32[5,32,96]{2,1,0:T(8,128)} %param.4), channel_id=2, replica_groups=mesh['y'=8,'x'=4,'zh'=4,'zl'=4,'c'=2] {'zh','zl'}, dimensions={0}, use_global_device_ids=true | all-gather | bytes 1044480 | tf_op jit(solution)/shard_map/all_gather | solution.py:54
  44.2 9.7 %collective-permute-start = (f32[16,5,32,96]{3,2,1,0:T(8,128)S(1)}, f32[16,5,32,96]{3,2,1,0:T(8,128)S(1)}, u32[]{:S(2)}, u32[]{:S(2)}) collective-permute-start(f32[16,5,32,96]{3,2,1,0:T(8,128)S(1)} %bitcast.3), channel_id=1, source_target_pairs={{0,1},{1,0},{2,3},{3,2},{4,5},{5,4},{6,7},{7,6},{8,9},{9,8},{10,11... | collective-permute-start | bytes 2949128 | tf_op jit(solution)/shard_map/ppermute | solution.py:55
  54.0 0.1 pad_add_fusion.where_ref
  54.1 2.6 %collective-permute-done.other_ref = f32[16,5,32,96]{3,2,1,0:T(8,128)S(1)} collective-permute-done((f32[16,5,32,96]{3,2,1,0:T(8,128)S(1)}, f32[16,5,32,96]{3,2,1,0:T(8,128)S(1)}, u32[]{:S(2)}, u32[]{:S(2)}) %collective-permute-start) | collective-permute-done | bytes 983072 | tf_op jit(solution)/shard_map/ppermute | solution.py:55
  56.6 0.0 copy-start
  56.6 1.8 %copy-done = f32[5,384,384]{2,1,0:T(8,128)S(1)} copy-done((f32[5,384,384]{2,1,0:T(8,128)S(1)}, f32[5,384,384]{2,1,0:T(8,128)}, u32[]{:S(2)}) %copy-start) | copy-done | bytes 2949144
  58.5 0.0 copy-start.1
  58.5 0.7 copy-done.1
  59.1 4.2 %shard_map.46 = f32[4,8,5,8,384]{4,3,2,1,0:T(8,128)S(1)} custom-call(s32[5]{0:T(128)S(1)} %copy-done.1, s32[2]{0:T(128)S(1)} %pad_add_fusion.where_ref, f32[16,5,32,96]{3,2,1,0:T(8,128)S(1)} %bitcast.4, f32[16,5,32,96]{3,2,1,0:T(8,128)S(1)} %collective-permute-done.other_ref, f32[5,384,384]{2,1,0:T(8,128)S(1)} %copy-done), custom_call_target="tpu_custom_call" | custom-call | flops 1200000000 | bytes 8000000 | tf_op jit(solution)/shard_map/pallas_call | solution.py:58
  63.3 27.9 %all_to_all.10 = f32[4,8,5,8,384]{4,3,2,1,0:T(8,128)S(1)} all-to-all(f32[4,8,5,8,384]{4,3,2,1,0:T(8,128)S(1)} %shard_map.46), channel_id=1, replica_groups=mesh['y'=8,'x'=4,'zh'=4,'zl'=4,'c'=2] {'x'}, dimensions={0} | all-to-all | bytes 3932160 | tf_op jit(solution)/shard_map/all_to_all | solution.py:72
  91.2 0.0 copy-start.3
  91.2 0.0 copy-start.2
  91.2 0.9 reduce_sum.18
  92.1 6.8 %all-to-all-start.1 = ((f32[8,5,8,384]{3,2,1,0:T(8,128)}), f32[8,5,8,384]{3,2,1,0:T(8,128)S(1)}, u32[]{:S(2)}, u32[]{:S(2)}) async-start(f32[8,5,8,384]{3,2,1,0:T(8,128)} %reduce_sum.18), calls=%async_computation.1 | async-start | bytes 983040 | tf_op jit(solution)/shard_map/all_to_all | solution.py:73
  99.0 0.0 copy-done.3
  99.0 0.1 broadcast_compare_fusion.1
  99.0 0.0 copy-done.2
  99.0 0.1 broadcast_compare_fusion
  99.1 14.5 %all-to-all-done.1 = f32[8,5,8,384]{3,2,1,0:T(8,128)S(1)} async-done(((f32[8,5,8,384]{3,2,1,0:T(8,128)}), f32[8,5,8,384]{3,2,1,0:T(8,128)S(1)}, u32[]{:S(2)}, u32[]{:S(2)}) %all-to-all-start.1) | async-done | bytes 491552 | tf_op jit(solution)/shard_map/all_to_all | solution.py:73
  113.7 0.7 and_select_fusion
  (3 shorter events, 0.0 us)
Async XLA Ops:
  44.2 12.4 %collective-permute-start = (f32[16,5,32,96]{3,2,1,0:T(8,128)S(1)}, f32[16,5,32,96]{3,2,1,0:T(8,128)S(1)}, u32[]{:S(2)}, u32[]{:S(2)}) collective-permute-start(f32[16,5,32,96]{3,2,1,0:T(8,128)S(1)} %bitcast.3), channel_id=1, source_target_pairs={{0,1},{1,0},{2,3},{3,2},{4,5},{5,4},{6,7},{7,6},{8,9},{9,8},{10,11... | collective-permute-start | bytes 2949128 | tf_op jit(solution)/shard_map/ppermute | solution.py:55
  56.6 1.8 %copy-start = (f32[5,384,384]{2,1,0:T(8,128)S(1)}, f32[5,384,384]{2,1,0:T(8,128)}, u32[]{:S(2)}) copy-start(f32[5,384,384]{2,1,0:T(8,128)} %integrals_ref.1) | copy-start | bytes 8847364
  58.5 0.7 copy-start.1
  91.2 7.8 %copy-start.3 = (s32[5]{0:T(128)S(1)}, s32[5]{0:T(128)}, u32[]{:S(2)}) copy-start(s32[5]{0:T(128)} %param.7) | copy-start | bytes 64
  91.2 7.9 %copy-start.2 = (s32[5]{0:T(128)S(1)}, s32[5]{0:T(128)}, u32[]{:S(2)}) copy-start(s32[5]{0:T(128)} %counts_ref.1) | copy-start | bytes 64
  92.1 21.5 %all-to-all-start.1 = ((f32[8,5,8,384]{3,2,1,0:T(8,128)}), f32[8,5,8,384]{3,2,1,0:T(8,128)S(1)}, u32[]{:S(2)}, u32[]{:S(2)}) async-start(f32[8,5,8,384]{3,2,1,0:T(8,128)} %reduce_sum.18), calls=%async_computation.1 | async-start | bytes 983040 | tf_op jit(solution)/shard_map/all_to_all | solution.py:73

commit v2 on v1

v2 whole, which is shorter than its diff:
```python
import functools

import jax
import jax.numpy as jnp
from jax import lax
from jax.experimental import pallas as pl
from jax.experimental.pallas import tpu as pltpu
from jax.sharding import Mesh
from jax.sharding import PartitionSpec as P

NX, YH, YL, ZH, ZL, CORES = 4, 4, 2, 4, 4, 2
BLOCKS, ROWS, PAIRS, COLS = 5, 32, 96, 384
LANES = 128
HALF = ZL * ROWS


def product(meta_ref, slab_ref, integrals_ref, *rest):
    out_ref, ahi, alo, bhi, blo, held, arrived = rest[-7:]
    g = pl.program_id(0)

    def fetch(block):
        return pltpu.make_async_copy(integrals_ref.at[block], held.at[block], arrived.at[block])

    @pl.when(g == 0)
    def _():
        for block in range(BLOCKS):
            fetch(block).start()
        for ref in (ahi, alo, bhi, blo):
            ref[...] = jnp.zeros_like(ref)

    left = meta_ref[g]
    lane = lax.broadcasted_iota(jnp.int32, (HALF, PAIRS), 1)
    for h in range(ZH):
        a = slab_ref[h * ZL:(h + 1) * ZL, 0].reshape(HALF, PAIRS)
        a = jnp.where(lane + h * PAIRS < left, a, 0.0)
        high = a.astype(jnp.bfloat16)
        ahi[:, h * LANES:h * LANES + PAIRS] = high
        alo[:, h * LANES:h * LANES + PAIRS] = (a - high.astype(jnp.float32)).astype(jnp.bfloat16)
    fetch(g).wait()
    for h in range(ZH):
        b = held[g, h * PAIRS:(h + 1) * PAIRS, :]
        high = b.astype(jnp.bfloat16)
        bhi[h * LANES:h * LANES + PAIRS, :] = high
        blo[h * LANES:h * LANES + PAIRS, :] = (b - high.astype(jnp.float32)).astype(jnp.bfloat16)
    dot = functools.partial(jnp.dot, preferred_element_type=jnp.float32)
    total = dot(ahi[...], bhi[...]) + (dot(ahi[...], blo[...]) + dot(alo[...], bhi[...]))
    for l in range(ZL):
        for x in range(NX):
            first = l * ROWS + x * 8
            out_ref[0, x, l, 0] = total[first:first + 8]


def partial_sums(meta, slab, integrals, filled=None):
    extra = [] if filled is None else [filled]
    return pl.pallas_call(
        product,
        out_shape=jax.ShapeDtypeStruct((YL, NX, YH, BLOCKS, 8, COLS), jnp.float32),
        grid_spec=pltpu.PrefetchScalarGridSpec(
            num_scalar_prefetch=1,
            grid=(BLOCKS,),
            in_specs=[
                pl.BlockSpec((ZH * ZL, 1, ROWS, PAIRS), lambda g, *_: (0, g, 0, 0)),
                pl.BlockSpec(memory_space=pltpu.HBM),
            ] + [pl.BlockSpec(memory_space=pl.ANY)] * len(extra),
            out_specs=pl.BlockSpec(
                (1, NX, YH, 1, 8, COLS), lambda g, meta: (meta[BLOCKS], 0, 0, g, 0, 0)
            ),
            scratch_shapes=[pltpu.VMEM((HALF, ZH * LANES), jnp.bfloat16)] * 2
            + [pltpu.VMEM((ZH * LANES, COLS), jnp.bfloat16)] * 2
            + [pltpu.VMEM((BLOCKS, COLS, COLS), jnp.float32), pltpu.SemaphoreType.DMA((BLOCKS,))],
        ),
        input_output_aliases={3: 0} if extra else {},
        compiler_params=pltpu.CompilerParams(vmem_limit_bytes=54_000_000),
        cost_estimate=pl.CostEstimate(flops=600_000_000, bytes_accessed=6_000_000, transcendentals=0),
    )(meta, slab, integrals, *extra)


def per_device(amplitudes, integrals, pair_counts, row_counts):
    y = lax.axis_index("yh") * YL + lax.axis_index("yl")
    gx = y * NX + lax.axis_index("x")
    core = lax.axis_index("c")
    own = lax.all_gather(amplitudes, ("zh", "zl"), axis=0, tiled=False)
    other = lax.ppermute(own, "c", [(0, 1), (1, 0)])
    left = pair_counts - gx * COLS
    filled = partial_sums(jnp.append(left, core), own, integrals)
    partial = partial_sums(jnp.append(left, 1 - core), other, integrals, filled)
    sent = partial.reshape(YL * NX, YH * BLOCKS * 8, COLS)
    near = lax.all_to_all(sent, ("yl", "x"), 0, 0, tiled=True).sum(0)
    far = lax.all_to_all(near.reshape(YH, BLOCKS * 8, COLS), "yh", 0, 0, tiled=True).sum(0)
    column_first = ((lax.axis_index("zh") * ZL + lax.axis_index("zl")) * CORES + core) * COLS
    column_used = column_first + lax.iota(jnp.int32, COLS)[None, :] < pair_counts[:, None]
    row_used = gx * 8 + lax.iota(jnp.int32, 8)[None, :] < row_counts[:, None]
    keep = jnp.logical_and(row_used[:, :, None], column_used[:, None, :])
    return jnp.where(keep, far.reshape(BLOCKS, 8, COLS), 0.0)


def solution(mesh):
    fine = Mesh(
        mesh.devices.reshape(YH, YL, NX, ZH, ZL, CORES), ("yh", "yl", "x", "zh", "zl", "c")
    )
    out = P(None, ("yh", "yl", "x"), ("zh", "zl", "c"))
    return jax.shard_map(
        per_device,
        mesh=fine,
        in_specs=(P(None, ("zl", "c"), ("yh", "yl", "x", "zh")), out, P(), P()),
        out_specs=out,
        check_vma=False,
    )
```

time: 115 us -> 112 us (0.974)
  blocking collectives: 72.1 us -> 44.2 us
  waiting for transfers between devices: 17.1 us -> 32.7 us
  Pallas kernels: 4.17 us -> 10.2 us
  starting transfers between devices: 16.6 us -> 20.7 us
  local copies, waits for them, and re-layouts: 2.49 us -> 0.01 us
    all_to_all x1 -> x0, blocking collectives: 27.9 us -> none  [per_device(): along_x = lax.all_to_all(partial, 'x', 0, 0, tiled=True).sum(0)]
    all_to_all x1 -> x2, waiting for transfers between devices: 14.5 us -> 32.7 us  [the longest x1 24.8 us: per_device(): near = lax.all_to_all(sent, ('yl', 'x'), 0, 0, tiled=True).sum(0)]
    pallas_call x1 -> x2, Pallas kernels: 4.17 us -> 10.2 us  [partial_sums(): pl.pallas_call(product, out_shape=jax.ShapeDtypeStruct((YL, NX, YH, BLOCK...]
    all_to_all x1 -> x2, starting transfers between devices: 6.83 us -> 11 us  [the longest x1 5.92 us: per_device(): lax.all_to_all(near.reshape(YH, BLOCKS * 8, COLS), 'yh', 0, 0, tiled=True)]
    ppermute x1, waiting for transfers between devices: 2.56 us -> 0.01 us  [per_device(): other = lax.ppermute(own, 'c', [(0, 1), (1, 0)])]
    unnamed x8 -> x4, local copies, waits for them, and re-layouts: 2.49 us -> 0.01 us
  transfers between devices with their start and end apart: 2 -> 3, of which waited for: 2 -> 2; matrix products, arithmetic and copies ran while one was open for 0% -> 1% of each run, Pallas kernels for 0% -> 5%
where the time goes in v2:
time: 112 us; the launch traced here: 110 us
  blocking collectives  44.2 us (39%)
  waiting for transfers between devices  32.7 us (29%)
  starting transfers between devices  20.7 us (18%)
  Pallas kernels  10.2 us (9%)
  other arithmetic  2.4 us (2%)
    all_gather x1, blocking collectives, per_device(): own = lax.all_gather(amplitudes, ('zh', 'zl'), axis=0, tiled=False)  44.2 us
    all_to_all x1, waiting for transfers between devices, per_device(): near = lax.all_to_all(sent, ('yl', 'x'), 0, 0, tiled=True).sum(0)  24.8 us
    pallas_call x2, Pallas kernels, partial_sums(): pl.pallas_call(product, out_shape=jax.ShapeDtypeStruct((YL, NX, YH, BLOCK...  10.2 us
    ppermute x1, starting transfers between devices, per_device(): other = lax.ppermute(own, 'c', [(0, 1), (1, 0)])  9.74 us
    all_to_all x1, waiting for transfers between devices, per_device(): lax.all_to_all(near.reshape(YH, BLOCKS * 8, COLS), 'yh', 0, 0, tiled=True)  7.89 us
    all_to_all x1, starting transfers between devices, per_device(): lax.all_to_all(near.reshape(YH, BLOCKS * 8, COLS), 'yh', 0, 0, tiled=True)  5.92 us
    all_to_all x1, starting transfers between devices, per_device(): near = lax.all_to_all(sent, ('yl', 'x'), 0, 0, tiled=True).sum(0)  5.04 us
  transfers between devices with their start and end apart: 3, of which 2 were waited for; matrix products, arithmetic and copies ran while one was open for 1% of the time, Pallas kernels for 5%

profile of v2, /device:TPU:1, one launch (start us, length us, event | category | flops | bytes accessed | tf_op | source)
XLA Modules:
  0.0 110.3 jit_solution(9898557338143917006)
XLA Ops:
  0.0 44.2 %all-gather = f32[80,32,96]{2,1,0:T(8,128)S(1)} all-gather(f32[5,32,96]{2,1,0:T(8,128)} %param.4), channel_id=2, replica_groups=mesh['yh'=4,'yl'=2,'x'=4,'zh'=4,'zl'=4,'c'=2] {'zh','zl'}, dimensions={0}, use_global_device_ids=true | all-gather | bytes 1044480 | tf_op jit(solution)/shard_map/all_gather | solution.py:82
  44.2 9.7 %collective-permute-start = (f32[16,5,32,96]{3,2,1,0:T(8,128)S(1)}, f32[16,5,32,96]{3,2,1,0:T(8,128)S(1)}, u32[]{:S(2)}, u32[]{:S(2)}) collective-permute-start(f32[16,5,32,96]{3,2,1,0:T(8,128)S(1)} %bitcast.7), channel_id=1, source_target_pairs={{0,1},{1,0},{2,3},{3,2},{4,5},{5,4},{6,7},{7,6},{8,9},{9,8},{10,11... | collective-permute-start | bytes 2949128 | tf_op jit(solution)/shard_map/ppermute | solution.py:83
  54.0 0.7 broadcast_subtract_fusion
  54.7 0.1 pad_add_fusion.1
  54.7 5.1 %shard_map.46.rest_0_ = f32[2,4,4,5,8,384]{5,4,3,2,1,0:T(8,128)} custom-call(s32[6]{0:T(128)S(1)} %get-tuple-element.5.meta_ref, f32[16,5,32,96]{3,2,1,0:T(8,128)S(1)} %bitcast.8, f32[5,384,384]{2,1,0:T(8,128)} %integrals_ref.3), custom_call_target="tpu_custom_call" | custom-call | flops 600000000 | bytes 6000000 | tf_op jit(solution)/shard_map/pallas_call | solution.py:55
  59.8 0.0 collective-permute-done.slab_ref
  59.8 5.1 %shard_map.47 = f32[2,4,4,5,8,384]{5,4,3,2,1,0:T(8,128)} custom-call(s32[6]{0:T(128)S(1)} %get-tuple-element.6.meta_ref, f32[16,5,32,96]{3,2,1,0:T(8,128)S(1)} %collective-permute-done.slab_ref, f32[5,384,384]{2,1,0:T(8,128)} %integrals_ref.3, f32[2,4,4,5,8,384]{5,4,3,2,1,0:T(8,128)} %shard_map.46.rest_0_), custom_call_target="tpu_custom_call", output_to_operand_aliasing={{}: (3, {})} | custom-call | flops 600000000 | bytes 6000000 | tf_op jit(solution)/shard_map/pallas_call | solution.py:55
  65.0 5.0 %all-to-all-start = ((f32[8,160,384]{2,1,0:T(8,128)}), f32[8,160,384]{2,1,0:T(8,128)S(1)}, u32[]{:S(2)}, u32[]{:S(2)}) async-start(f32[8,160,384]{2,1,0:T(8,128)} %bitcast.9), calls=%async_computation | async-start | bytes 3932160 | tf_op jit(solution)/shard_map/all_to_all | solution.py:88
  70.0 0.0 copy-start
  70.0 0.0 copy-start.1
  70.1 24.8 %all-to-all-done = f32[8,160,384]{2,1,0:T(8,128)S(1)} async-done(((f32[8,160,384]{2,1,0:T(8,128)}), f32[8,160,384]{2,1,0:T(8,128)S(1)}, u32[]{:S(2)}, u32[]{:S(2)}) %all-to-all-start) | async-done | bytes 1966112 | tf_op jit(solution)/shard_map/all_to_all | solution.py:88
  94.9 0.8 reduce_sum.18
  95.6 5.9 %all-to-all-start.1 = ((f32[4,40,384]{2,1,0:T(8,128)}), f32[4,40,384]{2,1,0:T(8,128)S(1)}, u32[]{:S(2)}, u32[]{:S(2)}) async-start(f32[4,40,384]{2,1,0:T(8,128)} %bitcast.4), calls=%async_computation.1 | async-start | bytes 491520 | tf_op jit(solution)/shard_map/all_to_all | solution.py:89
  101.6 0.0 copy-done
  101.6 0.1 broadcast_compare_fusion.1
  101.6 0.0 copy-done.1
  101.6 0.1 broadcast_compare_fusion
  101.7 7.9 %all-to-all-done.1 = f32[4,40,384]{2,1,0:T(8,128)S(1)} async-done(((f32[4,40,384]{2,1,0:T(8,128)}), f32[4,40,384]{2,1,0:T(8,128)S(1)}, u32[]{:S(2)}, u32[]{:S(2)}) %all-to-all-start.1) | async-done | bytes 245792 | tf_op jit(solution)/shard_map/all_to_all | solution.py:89
  109.6 0.7 bitcast_select_fusion
  (3 shorter events, 0.0 us)
Async XLA Ops:
  44.2 15.6 %collective-permute-start = (f32[16,5,32,96]{3,2,1,0:T(8,128)S(1)}, f32[16,5,32,96]{3,2,1,0:T(8,128)S(1)}, u32[]{:S(2)}, u32[]{:S(2)}) collective-permute-start(f32[16,5,32,96]{3,2,1,0:T(8,128)S(1)} %bitcast.7), channel_id=1, source_target_pairs={{0,1},{1,0},{2,3},{3,2},{4,5},{5,4},{6,7},{7,6},{8,9},{9,8},{10,11... | collective-permute-start | bytes 2949128 | tf_op jit(solution)/shard_map/ppermute | solution.py:83
  65.0 29.9 %all-to-all-start = ((f32[8,160,384]{2,1,0:T(8,128)}), f32[8,160,384]{2,1,0:T(8,128)S(1)}, u32[]{:S(2)}, u32[]{:S(2)}) async-start(f32[8,160,384]{2,1,0:T(8,128)} %bitcast.9), calls=%async_computation | async-start | bytes 3932160 | tf_op jit(solution)/shard_map/all_to_all | solution.py:88
  70.0 31.5 %copy-start = (s32[5]{0:T(128)S(1)}, s32[5]{0:T(128)}, u32[]{:S(2)}) copy-start(s32[5]{0:T(128)} %param.7) | copy-start | bytes 64
  70.0 31.6 %copy-start.1 = (s32[5]{0:T(128)S(1)}, s32[5]{0:T(128)}, u32[]{:S(2)}) copy-start(s32[5]{0:T(128)} %param.6) | copy-start | bytes 64
  95.6 14.0 %all-to-all-start.1 = ((f32[4,40,384]{2,1,0:T(8,128)}), f32[4,40,384]{2,1,0:T(8,128)S(1)}, u32[]{:S(2)}, u32[]{:S(2)}) async-start(f32[4,40,384]{2,1,0:T(8,128)} %bitcast.4), calls=%async_computation.1 | async-start | bytes 491520 | tf_op jit(solution)/shard_map/all_to_all | solution.py:89

commit v3 on v2

v3 whole, which is shorter than its diff:
```python
import functools

import jax
import jax.numpy as jnp
from jax import lax
from jax.experimental import pallas as pl
from jax.experimental.pallas import tpu as pltpu
from jax.sharding import Mesh
from jax.sharding import PartitionSpec as P

NX, NY, ZH, ZL, CORES = 4, 8, 4, 4, 2
BLOCKS, ROWS, PAIRS, COLS = 5, 32, 96, 384
LANES = 128
HALF = ZL * ROWS
FULL = CORES * HALF


def product(meta_ref, own_ref, other_ref, integrals_ref, *rest):
    outs, (a2, bhi, blo, total, held, arrived) = rest[:NX], rest[NX:]
    g = pl.program_id(0)

    def fetch(block):
        return pltpu.make_async_copy(integrals_ref.at[block], held.at[block], arrived.at[block])

    @pl.when(g == 0)
    def _():
        for block in range(BLOCKS):
            fetch(block).start()
        for ref in (a2, bhi, blo):
            ref[...] = jnp.zeros_like(ref)

    left, core, me = meta_ref[g], meta_ref[BLOCKS], meta_ref[BLOCKS + 1]
    lane = lax.broadcasted_iota(jnp.int32, (HALF, PAIRS), 1)
    for h in range(ZH):
        keep = lane + h * PAIRS < left
        at = slice(h * LANES, h * LANES + PAIRS)
        for part, ref in enumerate((own_ref, other_ref)):
            a = ref[h * ZL:(h + 1) * ZL, 0].reshape(HALF, PAIRS)
            a = jnp.where(keep, a, 0.0)
            high = a.astype(jnp.bfloat16)
            low = (a - high.astype(jnp.float32)).astype(jnp.bfloat16)
            a2[part * HALF:(part + 1) * HALF, at] = high
            a2[FULL + part * HALF:FULL + (part + 1) * HALF, at] = low
    fetch(g).wait()
    for h in range(ZH):
        b = held[g, h * PAIRS:(h + 1) * PAIRS, :]
        high = b.astype(jnp.bfloat16)
        bhi[h * LANES:h * LANES + PAIRS, :] = high
        blo[h * LANES:h * LANES + PAIRS, :] = (b - high.astype(jnp.float32)).astype(jnp.bfloat16)
    dot = functools.partial(jnp.dot, preferred_element_type=jnp.float32)
    both = dot(a2[...], bhi[...])
    total[...] = both[:FULL] + (both[FULL:] + dot(a2[:FULL], blo[...]))
    for step, out_ref in enumerate(outs):
        x = lax.rem(me + step, NX)
        for part in range(CORES):
            side = core if part == 0 else 1 - core
            for l in range(ZL):
                first = pl.multiple_of(part * HALF + l * ROWS + x * 8, 8)
                out_ref[2 * l + side, 0] = total[pl.ds(first, 8), :]


def partial_sums(meta, own, other, integrals):
    slab = pl.BlockSpec((ZH * ZL, 1, ROWS, PAIRS), lambda g, *_: (0, g, 0, 0))
    return pl.pallas_call(
        product,
        out_shape=[jax.ShapeDtypeStruct((NY, BLOCKS, 8, COLS), jnp.float32)] * NX,
        grid_spec=pltpu.PrefetchScalarGridSpec(
            num_scalar_prefetch=1,
            grid=(BLOCKS,),
            in_specs=[slab, slab, pl.BlockSpec(memory_space=pltpu.HBM)],
            out_specs=[pl.BlockSpec((NY, 1, 8, COLS), lambda g, *_: (0, g, 0, 0))] * NX,
            scratch_shapes=[
                pltpu.VMEM((2 * FULL, ZH * LANES), jnp.bfloat16),
                pltpu.VMEM((ZH * LANES, COLS), jnp.bfloat16),
                pltpu.VMEM((ZH * LANES, COLS), jnp.bfloat16),
                pltpu.VMEM((FULL, COLS), jnp.float32),
                pltpu.VMEM((BLOCKS, COLS, COLS), jnp.float32),
                pltpu.SemaphoreType.DMA((BLOCKS,)),
            ],
        ),
        compiler_params=pltpu.CompilerParams(vmem_limit_bytes=50_500_000),
        cost_estimate=pl.CostEstimate(flops=1_200_000_000, bytes_accessed=8_000_000, transcendentals=0),
    )(meta, own, other, integrals)


def per_device(amplitudes, integrals, pair_counts, row_counts):
    x = lax.axis_index("x")
    gx = lax.axis_index("y") * NX + x
    core = lax.axis_index("c")
    own = lax.all_gather(amplitudes, ("zh", "zl"), axis=0, tiled=False)
    other = lax.ppermute(own, "c", [(0, 1), (1, 0)])
    meta = jnp.concatenate([pair_counts - gx * COLS, jnp.stack([core, x])])
    near, *away = partial_sums(meta, own, other, integrals)
    for step in (2, 1, 3):
        ring = [(i, (i + step) % NX) for i in range(NX)]
        near = near + lax.ppermute(away[step - 1], "x", ring)
    far = lax.all_to_all(near.reshape(NY, BLOCKS * 8, COLS), "y", 0, 0, tiled=True).sum(0)
    column_first = ((lax.axis_index("zh") * ZL + lax.axis_index("zl")) * CORES + core) * COLS
    column_used = column_first + lax.iota(jnp.int32, COLS)[None, :] < pair_counts[:, None]
    row_used = gx * 8 + lax.iota(jnp.int32, 8)[None, :] < row_counts[:, None]
    keep = jnp.logical_and(row_used[:, :, None], column_used[:, None, :])
    return jnp.where(keep, far.reshape(BLOCKS, 8, COLS), 0.0)


def solution(mesh):
    fine = Mesh(mesh.devices.reshape(NY, NX, ZH, ZL, CORES), ("y", "x", "zh", "zl", "c"))
    out = P(None, ("y", "x"), ("zh", "zl", "c"))
    return jax.shard_map(
        per_device,
        mesh=fine,
        in_specs=(P(None, ("zl", "c"), ("y", "x", "zh")), out, P(), P()),
        out_specs=out,
        check_vma=False,
    )
```

time: 112 us -> 116 us (1.036)
  starting transfers between devices: 20.7 us -> 27.8 us
  Pallas kernels: 10.2 us -> 5.92 us
  waiting for transfers between devices: 32.7 us -> 35.5 us
    ppermute x0 -> x3, waiting for transfers between devices: none -> 15.9 us  [per_device(): near = near + lax.ppermute(away[step - 1], 'x', ring)]
    all_to_all x2 -> x1, waiting for transfers between devices: 32.7 us -> 17.1 us  [per_device(): lax.all_to_all(near.reshape(NY, BLOCKS * 8, COLS), 'y', 0, 0, tiled=True)]
    ppermute x0 -> x3, starting transfers between devices: none -> 11.2 us  [per_device(): near = near + lax.ppermute(away[step - 1], 'x', ring)]
    pallas_call x2 -> x1, Pallas kernels: 10.2 us -> 5.92 us  [partial_sums(): pl.pallas_call(product, out_shape=[jax.ShapeDtypeStruct((NY, BLOCKS, 8, C...]
    all_to_all x2 -> x1, starting transfers between devices: 11 us -> 6.83 us  [per_device(): lax.all_to_all(near.reshape(NY, BLOCKS * 8, COLS), 'y', 0, 0, tiled=True)]
    ppermute x1, waiting for transfers between devices: 0.01 us -> 2.53 us  [per_device(): other = lax.ppermute(own, 'c', [(0, 1), (1, 0)])]
  transfers between devices with their start and end apart: 3 -> 5, of which waited for: 2 -> 4; matrix products, arithmetic and copies ran while one was open for 1% -> 0% of each run, Pallas kernels for 5% -> 0%
where the time goes in v3:
time: 116 us; the launch traced here: 115 us
  blocking collectives  44.4 us (38%)
  waiting for transfers between devices  35.5 us (31%)
  starting transfers between devices  27.8 us (24%)
  Pallas kernels  5.92 us (5%)
  other arithmetic  1.86 us (2%)
    all_gather x1, blocking collectives, per_device(): own = lax.all_gather(amplitudes, ('zh', 'zl'), axis=0, tiled=False)  44.4 us
    all_to_all x1, waiting for transfers between devices, per_device(): lax.all_to_all(near.reshape(NY, BLOCKS * 8, COLS), 'y', 0, 0, tiled=True)  17.1 us
    ppermute x3, waiting for transfers between devices, per_device(): near = near + lax.ppermute(away[step - 1], 'x', ring)  15.9 us
    ppermute x3, starting transfers between devices, per_device(): near = near + lax.ppermute(away[step - 1], 'x', ring)  11.2 us
    ppermute x1, starting transfers between devices, per_device(): other = lax.ppermute(own, 'c', [(0, 1), (1, 0)])  9.74 us
    all_to_all x1, starting transfers between devices, per_device(): lax.all_to_all(near.reshape(NY, BLOCKS * 8, COLS), 'y', 0, 0, tiled=True)  6.83 us
    pallas_call x1, Pallas kernels, partial_sums(): pl.pallas_call(product, out_shape=[jax.ShapeDtypeStruct((NY, BLOCKS, 8, C...  5.92 us
    ppermute x1, waiting for transfers between devices, per_device(): other = lax.ppermute(own, 'c', [(0, 1), (1, 0)])  2.53 us
  transfers between devices with their start and end apart: 5, of which 4 were waited for; matrix products, arithmetic and copies ran while one was open for 0% of the time, Pallas kernels for 0%

profile of v3, /device:TPU:1, one launch (start us, length us, event | category | flops | bytes accessed | tf_op | source)
XLA Modules:
  0.0 115.5 jit_solution(10868576561660227993)
XLA Ops:
  0.0 0.0 copy-start.1
  0.0 44.4 %all-gather = f32[80,32,96]{2,1,0:T(8,128)S(1)} all-gather(f32[5,32,96]{2,1,0:T(8,128)} %param.4), channel_id=2, replica_groups=mesh['y'=8,'x'=4,'zh'=4,'zl'=4,'c'=2] {'zh','zl'}, dimensions={0}, use_global_device_ids=true | all-gather | bytes 1044480 | tf_op jit(solution)/shard_map/all_gather | solution.py:90
  44.4 9.7 %collective-permute-start = (f32[16,5,32,96]{3,2,1,0:T(8,128)S(1)}, f32[16,5,32,96]{3,2,1,0:T(8,128)S(1)}, u32[]{:S(2)}, u32[]{:S(2)}) collective-permute-start(f32[16,5,32,96]{3,2,1,0:T(8,128)S(1)} %bitcast.7), channel_id=1, source_target_pairs={{0,1},{1,0},{2,3},{3,2},{4,5},{5,4},{6,7},{7,6},{8,9},{9,8},{10,11... | collective-permute-start | bytes 2949128 | tf_op jit(solution)/shard_map/ppermute | solution.py:91
  54.1 0.0 copy-done.1
  54.2 0.1 pad_add_fusion.meta_ref
  54.2 2.5 %collective-permute-done.other_ref = f32[16,5,32,96]{3,2,1,0:T(8,128)S(1)} collective-permute-done((f32[16,5,32,96]{3,2,1,0:T(8,128)S(1)}, f32[16,5,32,96]{3,2,1,0:T(8,128)S(1)}, u32[]{:S(2)}, u32[]{:S(2)}) %collective-permute-start) | collective-permute-done | bytes 983072 | tf_op jit(solution)/shard_map/ppermute | solution.py:91
  56.8 5.9 %shard_map.46 = (f32[8,5,8,384]{3,2,1,0:T(8,128)S(1)}, f32[8,5,8,384]{3,2,1,0:T(8,128)S(1)}, f32[8,5,8,384]{3,2,1,0:T(8,128)S(1)}, f32[8,5,8,384]{3,2,1,0:T(8,128)S(1)}) custom-call(s32[7]{0:T(128)S(1)} %pad_add_fusion.meta_ref, f32[16,5,32,96]{3,2,1,0:T(8,128)S(1)} %bitcast.8, f32[16,5,32,96]{3,2,1,0:T(8,128)S(1)} %collective-permute-done.other_ref, ...), custom_call_target="tpu_custom_call" | custom-call | flops 1200000000 | bytes 8000000 | tf_op jit(solution)/shard_map/pallas_call | solution.py:64
  62.7 4.7 %collective-permute-start.1 = (f32[8,5,8,384]{3,2,1,0:T(8,128)S(1)}, f32[8,5,8,384]{3,2,1,0:T(8,128)S(1)}, u32[]{:S(2)}, u32[]{:S(2)}) collective-permute-start(f32[8,5,8,384]{3,2,1,0:T(8,128)S(1)} %get-tuple-element.10), channel_id=1, source_target_pairs={{0,64},{32,96},{64,0},{96,32},{1,65},{33,97},{65,1},{97,33},{2,66}... | collective-permute-start | bytes 1474568 | tf_op jit(solution)/shard_map/ppermute | solution.py:96
  67.4 2.2 %collective-permute-start.2 = (f32[8,5,8,384]{3,2,1,0:T(8,128)S(1)}, f32[8,5,8,384]{3,2,1,0:T(8,128)S(1)}, u32[]{:S(2)}, u32[]{:S(2)}) collective-permute-start(f32[8,5,8,384]{3,2,1,0:T(8,128)S(1)} %get-tuple-element.11), channel_id=1, source_target_pairs={{0,32},{32,64},{64,96},{96,0},{1,33},{33,65},{65,97},{97,1},{2,34}... | collective-permute-start | bytes 1474568 | tf_op jit(solution)/shard_map/ppermute | solution.py:96
  69.6 4.3 %collective-permute-start.3 = (f32[8,5,8,384]{3,2,1,0:T(8,128)S(1)}, f32[8,5,8,384]{3,2,1,0:T(8,128)S(1)}, u32[]{:S(2)}, u32[]{:S(2)}) collective-permute-start(f32[8,5,8,384]{3,2,1,0:T(8,128)S(1)} %get-tuple-element.12), channel_id=1, source_target_pairs={{0,96},{32,0},{64,32},{96,64},{1,97},{33,1},{65,33},{97,65},{2,98}... | collective-permute-start | bytes 1474568 | tf_op jit(solution)/shard_map/ppermute | solution.py:96
  73.9 4.7 %collective-permute-done.1 = f32[8,5,8,384]{3,2,1,0:T(8,128)S(1)} collective-permute-done((f32[8,5,8,384]{3,2,1,0:T(8,128)S(1)}, f32[8,5,8,384]{3,2,1,0:T(8,128)S(1)}, u32[]{:S(2)}, u32[]{:S(2)}) %collective-permute-start.1) | collective-permute-done | bytes 491552 | tf_op jit(solution)/shard_map/ppermute | solution.py:96
  78.6 11.2 %collective-permute-done.2 = f32[8,5,8,384]{3,2,1,0:T(8,128)S(1)} collective-permute-done((f32[8,5,8,384]{3,2,1,0:T(8,128)S(1)}, f32[8,5,8,384]{3,2,1,0:T(8,128)S(1)}, u32[]{:S(2)}, u32[]{:S(2)}) %collective-permute-start.2) | collective-permute-done | bytes 491552 | tf_op jit(solution)/shard_map/ppermute | solution.py:96
  89.8 0.0 collective-permute-done.3
  89.8 0.0 copy-start
  89.8 0.9 add_bitcast_fusion
  90.7 6.8 %all-to-all-start = ((f32[8,40,384]{2,1,0:T(8,128)}), f32[8,40,384]{2,1,0:T(8,128)S(1)}, u32[]{:S(2)}, u32[]{:S(2)}) async-start(f32[8,40,384]{2,1,0:T(8,128)} %add_bitcast_fusion), calls=%async_computation | async-start | bytes 983040 | tf_op jit(solution)/shard_map/all_to_all | solution.py:97
  97.5 0.0 copy-done
  97.5 0.1 broadcast_compare_fusion.1
  97.6 0.1 broadcast_compare_fusion
  97.7 17.1 %all-to-all-done = f32[8,40,384]{2,1,0:T(8,128)S(1)} async-done(((f32[8,40,384]{2,1,0:T(8,128)}), f32[8,40,384]{2,1,0:T(8,128)S(1)}, u32[]{:S(2)}, u32[]{:S(2)}) %all-to-all-start) | async-done | bytes 491552 | tf_op jit(solution)/shard_map/all_to_all | solution.py:97
  114.8 0.7 bitcast_select_fusion
  (4 shorter events, 0.0 us)
Async XLA Ops:
  0.0 54.1 %copy-start.1 = (s32[5]{0:T(128)S(1)}, s32[5]{0:T(128)}, u32[]{:S(2)}) copy-start(s32[5]{0:T(128)} %param.6) | copy-start | bytes 64
  44.4 12.4 %collective-permute-start = (f32[16,5,32,96]{3,2,1,0:T(8,128)S(1)}, f32[16,5,32,96]{3,2,1,0:T(8,128)S(1)}, u32[]{:S(2)}, u32[]{:S(2)}) collective-permute-start(f32[16,5,32,96]{3,2,1,0:T(8,128)S(1)} %bitcast.7), channel_id=1, source_target_pairs={{0,1},{1,0},{2,3},{3,2},{4,5},{5,4},{6,7},{7,6},{8,9},{9,8},{10,11... | collective-permute-start | bytes 2949128 | tf_op jit(solution)/shard_map/ppermute | solution.py:91
  62.7 15.9 %collective-permute-start.1 = (f32[8,5,8,384]{3,2,1,0:T(8,128)S(1)}, f32[8,5,8,384]{3,2,1,0:T(8,128)S(1)}, u32[]{:S(2)}, u32[]{:S(2)}) collective-permute-start(f32[8,5,8,384]{3,2,1,0:T(8,128)S(1)} %get-tuple-element.10), channel_id=1, source_target_pairs={{0,64},{32,96},{64,0},{96,32},{1,65},{33,97},{65,1},{97,33},{2,66}... | collective-permute-start | bytes 1474568 | tf_op jit(solution)/shard_map/ppermute | solution.py:96
  67.4 22.4 %collective-permute-start.2 = (f32[8,5,8,384]{3,2,1,0:T(8,128)S(1)}, f32[8,5,8,384]{3,2,1,0:T(8,128)S(1)}, u32[]{:S(2)}, u32[]{:S(2)}) collective-permute-start(f32[8,5,8,384]{3,2,1,0:T(8,128)S(1)} %get-tuple-element.11), channel_id=1, source_target_pairs={{0,32},{32,64},{64,96},{96,0},{1,33},{33,65},{65,97},{97,1},{2,34}... | collective-permute-start | bytes 1474568 | tf_op jit(solution)/shard_map/ppermute | solution.py:96
  69.6 20.1 %collective-permute-start.3 = (f32[8,5,8,384]{3,2,1,0:T(8,128)S(1)}, f32[8,5,8,384]{3,2,1,0:T(8,128)S(1)}, u32[]{:S(2)}, u32[]{:S(2)}) collective-permute-start(f32[8,5,8,384]{3,2,1,0:T(8,128)S(1)} %get-tuple-element.12), channel_id=1, source_target_pairs={{0,96},{32,0},{64,32},{96,64},{1,97},{33,1},{65,33},{97,65},{2,98}... | collective-permute-start | bytes 1474568 | tf_op jit(solution)/shard_map/ppermute | solution.py:96
  89.8 7.7 %copy-start = (s32[5]{0:T(128)S(1)}, s32[5]{0:T(128)}, u32[]{:S(2)}) copy-start(s32[5]{0:T(128)} %param.7) | copy-start | bytes 64
  90.7 24.1 %all-to-all-start = ((f32[8,40,384]{2,1,0:T(8,128)}), f32[8,40,384]{2,1,0:T(8,128)S(1)}, u32[]{:S(2)}, u32[]{:S(2)}) async-start(f32[8,40,384]{2,1,0:T(8,128)} %add_bitcast_fusion), calls=%async_computation | async-start | bytes 983040 | tf_op jit(solution)/shard_map/all_to_all | solution.py:97

commit v4 on v2

v4 whole, which is shorter than its diff:
```python
import functools

import jax
import jax.numpy as jnp
from jax import lax
from jax.experimental import pallas as pl
from jax.experimental.pallas import tpu as pltpu
from jax.sharding import Mesh
from jax.sharding import PartitionSpec as P

NX, YH, YL, ZH, ZL, CORES = 4, 4, 2, 4, 4, 2
BLOCKS, ROWS, PAIRS, COLS = 5, 32, 96, 384
LANES = 128
HALF = ZL * ROWS
FULL = CORES * HALF
LIMIT = 24 * 1024 * 1024


def split(integrals_ref, bhi_ref, blo_ref):
    pad = jnp.zeros((LANES - PAIRS, COLS), jnp.bfloat16)
    for h in range(ZH):
        b = integrals_ref[0, h * PAIRS:(h + 1) * PAIRS, :]
        high = b.astype(jnp.bfloat16)
        low = (b - high.astype(jnp.float32)).astype(jnp.bfloat16)
        for ref, value in ((bhi_ref, high), (blo_ref, low)):
            ref[0, h * LANES:h * LANES + PAIRS, :] = value
            ref[0, h * LANES + PAIRS:(h + 1) * LANES, :] = pad


def split_integrals(integrals):
    halves = pl.BlockSpec((1, ZH * LANES, COLS), lambda g: (g, 0, 0))
    return pl.pallas_call(
        split,
        out_shape=[jax.ShapeDtypeStruct((BLOCKS, ZH * LANES, COLS), jnp.bfloat16)] * 2,
        grid=(BLOCKS,),
        in_specs=[pl.BlockSpec((1, COLS, COLS), lambda g: (g, 0, 0))],
        out_specs=[halves, halves],
        compiler_params=pltpu.CompilerParams(vmem_limit_bytes=LIMIT),
        cost_estimate=pl.CostEstimate(flops=5_000_000, bytes_accessed=7_000_000, transcendentals=0),
    )(integrals)


def product(meta_ref, own_ref, other_ref, bhi_ref, blo_ref, out_ref, ahi, alo):
    for h in range(ZH):
        pad = slice(h * LANES + PAIRS, (h + 1) * LANES)
        for ref in (ahi, alo):
            ref[:, :, pad] = jnp.zeros((2, FULL, LANES - PAIRS), jnp.bfloat16)

    core = meta_ref[BLOCKS]
    lane = lax.broadcasted_iota(jnp.int32, (HALF, PAIRS), 1)
    dot = functools.partial(jnp.dot, preferred_element_type=jnp.float32)
    for g in range(BLOCKS):
        slot = g % 2
        left = meta_ref[g]
        for h in range(ZH):
            keep = lane < left - h * PAIRS
            at = slice(h * LANES, h * LANES + PAIRS)
            for part, ref in enumerate((own_ref, other_ref)):
                rows = slice(part * HALF, (part + 1) * HALF)
                a = ref[h * ZL:(h + 1) * ZL, g].reshape(HALF, PAIRS)
                a = jnp.where(keep, a, 0.0)
                high = a.astype(jnp.bfloat16)
                ahi[slot, rows, at] = high
                alo[slot, rows, at] = (a - high.astype(jnp.float32)).astype(jnp.bfloat16)
        total = dot(ahi[slot], bhi_ref[g]) + (dot(ahi[slot], blo_ref[g]) + dot(alo[slot], bhi_ref[g]))
        for part in range(CORES):
            side = core if part == 0 else 1 - core
            for l in range(ZL):
                for x in range(NX):
                    first = part * HALF + l * ROWS + x * 8
                    out_ref[side, x, l, g] = total[first:first + 8]


def partial_sums(meta, own, other, integrals):
    whole = pl.BlockSpec(memory_space=pltpu.VMEM)
    bhi, blo = split_integrals(integrals)
    return pl.pallas_call(
        product,
        out_shape=jax.ShapeDtypeStruct((YL, NX, YH, BLOCKS, 8, COLS), jnp.float32),
        in_specs=[pl.BlockSpec(memory_space=pltpu.SMEM)] + [whole] * 4,
        out_specs=whole,
        scratch_shapes=[pltpu.VMEM((2, FULL, ZH * LANES), jnp.bfloat16)] * 2,
        compiler_params=pltpu.CompilerParams(vmem_limit_bytes=LIMIT),
        cost_estimate=pl.CostEstimate(flops=1_200_000_000, bytes_accessed=8_000_000, transcendentals=0),
    )(meta, own, other, bhi, blo)


def per_device(amplitudes, integrals, pair_counts, row_counts):
    y = lax.axis_index("yh") * YL + lax.axis_index("yl")
    gx = y * NX + lax.axis_index("x")
    core = lax.axis_index("c")
    own = lax.all_gather(amplitudes, ("zh", "zl"), axis=0, tiled=False)
    other = lax.ppermute(own, "c", [(0, 1), (1, 0)])
    partial = partial_sums(jnp.append(pair_counts - gx * COLS, core), own, other, integrals)
    sent = partial.reshape(YL * NX, YH * BLOCKS * 8, COLS)
    near = lax.all_to_all(sent, ("yl", "x"), 0, 0, tiled=True).sum(0)
    far = lax.all_to_all(near.reshape(YH, BLOCKS * 8, COLS), "yh", 0, 0, tiled=True).sum(0)
    column_first = ((lax.axis_index("zh") * ZL + lax.axis_index("zl")) * CORES + core) * COLS
    column_used = column_first + lax.iota(jnp.int32, COLS)[None, :] < pair_counts[:, None]
    row_used = gx * 8 + lax.iota(jnp.int32, 8)[None, :] < row_counts[:, None]
    keep = jnp.logical_and(row_used[:, :, None], column_used[:, None, :])
    return jnp.where(keep, far.reshape(BLOCKS, 8, COLS), 0.0)


def solution(mesh):
    fine = Mesh(
        mesh.devices.reshape(YH, YL, NX, ZH, ZL, CORES), ("yh", "yl", "x", "zh", "zl", "c")
    )
    out = P(None, ("yh", "yl", "x"), ("zh", "zl", "c"))
    return jax.shard_map(
        per_device,
        mesh=fine,
        in_specs=(P(None, ("zl", "c"), ("yh", "yl", "x", "zh")), out, P(), P()),
        out_specs=out,
        check_vma=False,
    )
```

time: 112 us -> 108 us (0.964)
  Pallas kernels: 10.2 us -> 5.03 us
  local copies, waits for them, and re-layouts: 0.01 us -> 1.84 us
    pallas_call x2 -> x1, Pallas kernels: 10.2 us -> 4.51 us  [partial_sums(): pl.pallas_call(product, out_shape=jax.ShapeDtypeStruct((YL, NX, YH, BLOCK...]
    unnamed x4 -> x6, local copies, waits for them, and re-layouts: 0.01 us -> 1.84 us
  transfers between devices with their start and end apart: 3 -> 3, of which waited for: 2 -> 3; matrix products, arithmetic and copies ran while one was open for 1% -> 0% of each run, Pallas kernels for 5% -> 0%
where the time goes in v4:
time: 108 us; the launch traced here: 107 us
  blocking collectives  44.4 us (41%)
  waiting for transfers between devices  32.8 us (30%)
  starting transfers between devices  20.7 us (19%)
  Pallas kernels  5.03 us (5%)
  local copies, waits for them, and re-layouts  1.84 us (2%)
  other arithmetic  1.75 us (2%)
    all_gather x1, blocking collectives, per_device(): own = lax.all_gather(amplitudes, ('zh', 'zl'), axis=0, tiled=False)  44.4 us
    all_to_all x1, waiting for transfers between devices, per_device(): near = lax.all_to_all(sent, ('yl', 'x'), 0, 0, tiled=True).sum(0)  24.8 us
    ppermute x1, starting transfers between devices, per_device(): other = lax.ppermute(own, 'c', [(0, 1), (1, 0)])  9.74 us
    all_to_all x1, waiting for transfers between devices, per_device(): lax.all_to_all(near.reshape(YH, BLOCKS * 8, COLS), 'yh', 0, 0, tiled=True)  7.89 us
    all_to_all x1, starting transfers between devices, per_device(): lax.all_to_all(near.reshape(YH, BLOCKS * 8, COLS), 'yh', 0, 0, tiled=True)  5.92 us
    all_to_all x1, starting transfers between devices, per_device(): near = lax.all_to_all(sent, ('yl', 'x'), 0, 0, tiled=True).sum(0)  5.03 us
    pallas_call x1, Pallas kernels, partial_sums(): pl.pallas_call(product, out_shape=jax.ShapeDtypeStruct((YL, NX, YH, BLOCK...  4.51 us
  transfers between devices with their start and end apart: 3, of which 3 were waited for; matrix products, arithmetic and copies ran while one was open for 0% of the time, Pallas kernels for 0%

profile of v4, /device:TPU:1, one launch (start us, length us, event | category | flops | bytes accessed | tf_op | source)
XLA Modules:
  0.0 106.6 jit_solution(3527262287211339730)
XLA Ops:
  0.0 0.0 copy-start.2
  0.0 44.4 %all-gather = f32[80,32,96]{2,1,0:T(8,128)S(1)} all-gather(f32[5,32,96]{2,1,0:T(8,128)} %param.4), channel_id=2, replica_groups=mesh['yh'=4,'yl'=2,'x'=4,'zh'=4,'zl'=4,'c'=2] {'zh','zl'}, dimensions={0}, use_global_device_ids=true | all-gather | bytes 1044480 | tf_op jit(solution)/shard_map/all_gather | solution.py:92
  44.4 9.7 %collective-permute-start = (f32[16,5,32,96]{3,2,1,0:T(8,128)S(1)}, f32[16,5,32,96]{3,2,1,0:T(8,128)S(1)}, u32[]{:S(2)}, u32[]{:S(2)}) collective-permute-start(f32[16,5,32,96]{3,2,1,0:T(8,128)S(1)} %bitcast.6), channel_id=1, source_target_pairs={{0,1},{1,0},{2,3},{3,2},{4,5},{5,4},{6,7},{7,6},{8,9},{9,8},{10,11... | collective-permute-start | bytes 2949128 | tf_op jit(solution)/shard_map/ppermute | solution.py:93
  54.1 0.0 copy-start
  54.1 1.8 %copy-done = f32[5,384,384]{2,1,0:T(8,128)S(1)} copy-done((f32[5,384,384]{2,1,0:T(8,128)S(1)}, f32[5,384,384]{2,1,0:T(8,128)}, u32[]{:S(2)}) %copy-start) | copy-done | bytes 2949144
  56.0 0.5 shard_map.46
  56.5 0.0 copy-done.2
  56.5 0.1 pad_add_fusion.meta_ref
  56.6 0.2 collective-permute-done.other_ref
  56.8 4.5 %shard_map.47 = f32[2,4,4,5,8,384]{5,4,3,2,1,0:T(8,128)} custom-call(s32[6]{0:T(128)S(1)} %pad_add_fusion.meta_ref, f32[16,5,32,96]{3,2,1,0:T(8,128)S(1)} %bitcast.7, f32[16,5,32,96]{3,2,1,0:T(8,128)S(1)} %collective-permute-done.other_ref, bf16[5,512,384]{2,1,0:T(8,128)(2,1)S(1)} %get-tuple-element.7.bhi_ref, bf16[5,512,384]{2,1,0:T(8,128)(2,1)S(1)} %get-tuple-element.8.blo_ref), custom_call_target="tpu_custom_call" | custom-call | flops 1200000000 | bytes 8000000 | tf_op jit(solution)/shard_map/pallas_call | solution.py:77
  61.3 5.0 %all-to-all-start = ((f32[8,160,384]{2,1,0:T(8,128)}), f32[8,160,384]{2,1,0:T(8,128)S(1)}, u32[]{:S(2)}, u32[]{:S(2)}) async-start(f32[8,160,384]{2,1,0:T(8,128)} %bitcast.2), calls=%async_computation | async-start | bytes 3932160 | tf_op jit(solution)/shard_map/all_to_all | solution.py:96
  66.3 0.0 copy-start.1
  66.3 24.8 %all-to-all-done = f32[8,160,384]{2,1,0:T(8,128)S(1)} async-done(((f32[8,160,384]{2,1,0:T(8,128)}), f32[8,160,384]{2,1,0:T(8,128)S(1)}, u32[]{:S(2)}, u32[]{:S(2)}) %all-to-all-start) | async-done | bytes 1966112 | tf_op jit(solution)/shard_map/all_to_all | solution.py:96
  91.1 0.8 reduce_sum.18
  91.9 5.9 %all-to-all-start.1 = ((f32[4,40,384]{2,1,0:T(8,128)}), f32[4,40,384]{2,1,0:T(8,128)S(1)}, u32[]{:S(2)}, u32[]{:S(2)}) async-start(f32[4,40,384]{2,1,0:T(8,128)} %bitcast.3), calls=%async_computation.1 | async-start | bytes 491520 | tf_op jit(solution)/shard_map/all_to_all | solution.py:97
  97.8 0.0 copy-done.1
  97.8 0.1 broadcast_compare_fusion.1
  97.9 0.1 broadcast_compare_fusion
  98.0 7.9 %all-to-all-done.1 = f32[4,40,384]{2,1,0:T(8,128)S(1)} async-done(((f32[4,40,384]{2,1,0:T(8,128)}), f32[4,40,384]{2,1,0:T(8,128)S(1)}, u32[]{:S(2)}, u32[]{:S(2)}) %all-to-all-start.1) | async-done | bytes 245792 | tf_op jit(solution)/shard_map/all_to_all | solution.py:97
  105.9 0.7 bitcast_select_fusion
  (4 shorter events, 0.0 us)
Async XLA Ops:
  0.0 56.5 %copy-start.2 = (s32[5]{0:T(128)S(1)}, s32[5]{0:T(128)}, u32[]{:S(2)}) copy-start(s32[5]{0:T(128)} %param.6) | copy-start | bytes 64
  44.4 12.4 %collective-permute-start = (f32[16,5,32,96]{3,2,1,0:T(8,128)S(1)}, f32[16,5,32,96]{3,2,1,0:T(8,128)S(1)}, u32[]{:S(2)}, u32[]{:S(2)}) collective-permute-start(f32[16,5,32,96]{3,2,1,0:T(8,128)S(1)} %bitcast.6), channel_id=1, source_target_pairs={{0,1},{1,0},{2,3},{3,2},{4,5},{5,4},{6,7},{7,6},{8,9},{9,8},{10,11... | collective-permute-start | bytes 2949128 | tf_op jit(solution)/shard_map/ppermute | solution.py:93
  54.1 1.8 %copy-start = (f32[5,384,384]{2,1,0:T(8,128)S(1)}, f32[5,384,384]{2,1,0:T(8,128)}, u32[]{:S(2)}) copy-start(f32[5,384,384]{2,1,0:T(8,128)} %integrals_ref.1) | copy-start | bytes 8847364
  61.3 29.8 %all-to-all-start = ((f32[8,160,384]{2,1,0:T(8,128)}), f32[8,160,384]{2,1,0:T(8,128)S(1)}, u32[]{:S(2)}, u32[]{:S(2)}) async-start(f32[8,160,384]{2,1,0:T(8,128)} %bitcast.2), calls=%async_computation | async-start | bytes 3932160 | tf_op jit(solution)/shard_map/all_to_all | solution.py:96
  66.3 31.5 %copy-start.1 = (s32[5]{0:T(128)S(1)}, s32[5]{0:T(128)}, u32[]{:S(2)}) copy-start(s32[5]{0:T(128)} %param.7) | copy-start | bytes 64
  91.9 14.0 %all-to-all-start.1 = ((f32[4,40,384]{2,1,0:T(8,128)}), f32[4,40,384]{2,1,0:T(8,128)S(1)}, u32[]{:S(2)}, u32[]{:S(2)}) async-start(f32[4,40,384]{2,1,0:T(8,128)} %bitcast.3), calls=%async_computation.1 | async-start | bytes 491520 | tf_op jit(solution)/shard_map/all_to_all | solution.py:97

commit v5 on v4

--- a/solution.py
+++ b/solution.py
@@ -11,6 +11,7 @@
 NX, YH, YL, ZH, ZL, CORES = 4, 4, 2, 4, 4, 2
 BLOCKS, ROWS, PAIRS, COLS = 5, 32, 96, 384
 LANES = 128
+PACKED = ROWS * PAIRS // LANES
 HALF = ZL * ROWS
 FULL = CORES * HALF
 LIMIT = 24 * 1024 * 1024
@@ -40,13 +41,29 @@
     )(integrals)
 
 
-def product(meta_ref, own_ref, other_ref, bhi_ref, blo_ref, out_ref, ahi, alo):
+def pack(amplitudes):
+    third = LANES - PAIRS
+    last = [amplitudes[:, PACKED:, i * third:(i + 1) * third] for i in range(3)]
+    return jnp.concatenate([amplitudes[:, :PACKED], jnp.concatenate(last, axis=1)], axis=2)
+
+
+def unpack(rows):
+    last = [rows[:, i * 8:(i + 1) * 8, PAIRS:] for i in range(3)]
+    return jnp.concatenate([rows[:, :, :PAIRS], jnp.concatenate(last, axis=2)], axis=1)
+
+
+def product(meta_ref, own_ref, other_ref, bhi_ref, blo_ref, out_ref, ahi, alo, result, sent):
+    core = meta_ref[BLOCKS]
+
+    def send(g, part):
+        side = core if part == 0 else 1 - core
+        return pltpu.make_async_copy(result.at[g, part], out_ref.at[side, :, :, g], sent.at[g, part])
+
     for h in range(ZH):
         pad = slice(h * LANES + PAIRS, (h + 1) * LANES)
         for ref in (ahi, alo):
             ref[:, :, pad] = jnp.zeros((2, FULL, LANES - PAIRS), jnp.bfloat16)
 
-    core = meta_ref[BLOCKS]
     lane = lax.broadcasted_iota(jnp.int32, (HALF, PAIRS), 1)
     dot = functools.partial(jnp.dot, preferred_element_type=jnp.float32)
     for g in range(BLOCKS):
@@ -57,18 +74,21 @@
             at = slice(h * LANES, h * LANES + PAIRS)
             for part, ref in enumerate((own_ref, other_ref)):
                 rows = slice(part * HALF, (part + 1) * HALF)
-                a = ref[h * ZL:(h + 1) * ZL, g].reshape(HALF, PAIRS)
+                a = unpack(ref[h * ZL:(h + 1) * ZL, g]).reshape(HALF, PAIRS)
                 a = jnp.where(keep, a, 0.0)
                 high = a.astype(jnp.bfloat16)
                 ahi[slot, rows, at] = high
                 alo[slot, rows, at] = (a - high.astype(jnp.float32)).astype(jnp.bfloat16)
         total = dot(ahi[slot], bhi_ref[g]) + (dot(ahi[slot], blo_ref[g]) + dot(alo[slot], bhi_ref[g]))
         for part in range(CORES):
-            side = core if part == 0 else 1 - core
             for l in range(ZL):
                 for x in range(NX):
                     first = part * HALF + l * ROWS + x * 8
-                    out_ref[side, x, l, g] = total[first:first + 8]
+                    result[g, part, x, l] = total[first:first + 8]
+            send(g, part).start()
+    for g in range(BLOCKS):
+        for part in range(CORES):
+            send(g, part).wait()
 
 
 def partial_sums(meta, own, other, integrals):
@@ -78,8 +98,12 @@
         product,
         out_shape=jax.ShapeDtypeStruct((YL, NX, YH, BLOCKS, 8, COLS), jnp.float32),
         in_specs=[pl.BlockSpec(memory_space=pltpu.SMEM)] + [whole] * 4,
-        out_specs=whole,
-        scratch_shapes=[pltpu.VMEM((2, FULL, ZH * LANES), jnp.bfloat16)] * 2,
+        out_specs=pl.BlockSpec(memory_space=pltpu.HBM),
+        scratch_shapes=[pltpu.VMEM((2, FULL, ZH * LANES), jnp.bfloat16)] * 2
+        + [
+            pltpu.VMEM((BLOCKS, CORES, NX, YH, 8, COLS), jnp.float32),
+            pltpu.SemaphoreType.DMA((BLOCKS, CORES)),
+        ],
         compiler_params=pltpu.CompilerParams(vmem_limit_bytes=LIMIT),
         cost_estimate=pl.CostEstimate(flops=1_200_000_000, bytes_accessed=8_000_000, transcendentals=0),
     )(meta, own, other, bhi, blo)
@@ -89,7 +113,7 @@
     y = lax.axis_index("yh") * YL + lax.axis_index("yl")
     gx = y * NX + lax.axis_index("x")
     core = lax.axis_index("c")
-    own = lax.all_gather(amplitudes, ("zh", "zl"), axis=0, tiled=False)
+    own = lax.all_gather(pack(amplitudes), ("zh", "zl"), axis=0, tiled=False)
     other = lax.ppermute(own, "c", [(0, 1), (1, 0)])
     partial = partial_sums(jnp.append(pair_counts - gx * COLS, core), own, other, integrals)
     sent = partial.reshape(YL * NX, YH * BLOCKS * 8, COLS)

time: 108 us -> 107 us (level)
  blocking collectives: 44.4 us -> 41.9 us
  local copies, waits for them, and re-layouts: 1.84 us -> 3.59 us
    all_gather x1, blocking collectives: 44.4 us -> 41.9 us  [per_device(): own = lax.all_gather(pack(amplitudes), ('zh', 'zl'), axis=0, tiled=False)]
    slice x0 -> x2, local copies, waits for them, and re-layouts: none -> 1.75 us  [the longest x1 0.91 us: pack(): last = [amplitudes[:, PACKED:, i * third:(i + 1) * third] for i in range(3)]]
  transfers between devices with their start and end apart: 3 -> 3, of which waited for: 3 -> 2; matrix products, arithmetic and copies ran while one was open for 0% -> 0% of each run, Pallas kernels for 0% -> 0%
where the time goes in v5:
time: 107 us; the launch traced here: 105 us
  blocking collectives  41.9 us (39%)
  waiting for transfers between devices  32.7 us (31%)
  starting transfers between devices  20.4 us (19%)
  Pallas kernels  4.39 us (4%)
  local copies, waits for them, and re-layouts  3.59 us (3%)
  other arithmetic  1.84 us (2%)
    all_gather x1, blocking collectives, per_device(): own = lax.all_gather(pack(amplitudes), ('zh', 'zl'), axis=0, tiled=False)  41.9 us
    all_to_all x1, waiting for transfers between devices, per_device(): near = lax.all_to_all(sent, ('yl', 'x'), 0, 0, tiled=True).sum(0)  24.8 us
    ppermute x1, starting transfers between devices, per_device(): other = lax.ppermute(own, 'c', [(0, 1), (1, 0)])  9.49 us
    all_to_all x1, waiting for transfers between devices, per_device(): lax.all_to_all(near.reshape(YH, BLOCKS * 8, COLS), 'yh', 0, 0, tiled=True)  7.89 us
    all_to_all x1, starting transfers between devices, per_device(): lax.all_to_all(near.reshape(YH, BLOCKS * 8, COLS), 'yh', 0, 0, tiled=True)  5.91 us
    all_to_all x1, starting transfers between devices, per_device(): near = lax.all_to_all(sent, ('yl', 'x'), 0, 0, tiled=True).sum(0)  5.05 us
    pallas_call x1, Pallas kernels, partial_sums(): pl.pallas_call(product, out_shape=jax.ShapeDtypeStruct((YL, NX, YH, BLOCK...  3.87 us
  transfers between devices with their start and end apart: 3, of which 2 were waited for; matrix products, arithmetic and copies ran while one was open for 0% of the time, Pallas kernels for 0%

profile of v5, /device:TPU:1, one launch (start us, length us, event | category | flops | bytes accessed | tf_op | source)
XLA Modules:
  0.0 105.0 jit_solution(361768633565017509)
XLA Ops:
  0.0 0.9 fusion
  0.9 0.8 slice.12
  1.8 0.1 maximum_maximum_fusion
  1.8 0.0 copy-start.2
  1.9 41.9 %all-gather = f32[80,24,128]{2,1,0:T(8,128)S(1)} all-gather(f32[5,24,128]{2,1,0:T(8,128)S(1)} %maximum_maximum_fusion), channel_id=2, replica_groups=mesh['yh'=4,'yl'=2,'x'=4,'zh'=4,'zl'=4,'c'=2] {'zh','zl'}, dimensions={0}, use_global_device_ids=true | all-gather | bytes 1044480 | tf_op jit(solution)/shard_map/all_gather | solution.py:116
  43.8 9.5 %collective-permute-start = (f32[16,5,24,128]{3,2,1,0:T(8,128)S(1)}, f32[16,5,24,128]{3,2,1,0:T(8,128)S(1)}, u32[]{:S(2)}, u32[]{:S(2)}) collective-permute-start(f32[16,5,24,128]{3,2,1,0:T(8,128)S(1)} %bitcast.6), channel_id=1, source_target_pairs={{0,1},{1,0},{2,3},{3,2},{4,5},{5,4},{6,7},{7,6},{8,9},{9,8},{10,11... | collective-permute-start | bytes 2949128 | tf_op jit(solution)/shard_map/ppermute | solution.py:117
  53.3 0.0 copy-start
  53.3 1.8 %copy-done = f32[5,384,384]{2,1,0:T(8,128)S(1)} copy-done((f32[5,384,384]{2,1,0:T(8,128)S(1)}, f32[5,384,384]{2,1,0:T(8,128)}, u32[]{:S(2)}) %copy-start) | copy-done | bytes 2949144
  55.1 0.5 shard_map.46
  55.6 0.0 copy-done.2
  55.7 0.1 pad_add_fusion.meta_ref
  55.7 0.0 collective-permute-done.other_ref
  55.8 3.9 %shard_map.47 = f32[2,4,4,5,8,384]{5,4,3,2,1,0:T(8,128)} custom-call(s32[6]{0:T(128)S(1)} %pad_add_fusion.meta_ref, f32[16,5,24,128]{3,2,1,0:T(8,128)S(1)} %bitcast.7, f32[16,5,24,128]{3,2,1,0:T(8,128)S(1)} %collective-permute-done.other_ref, bf16[5,512,384]{2,1,0:T(8,128)(2,1)S(1)} %get-tuple-element.7.bhi_ref, ...), custom_call_target="tpu_custom_call" | custom-call | flops 1200000000 | bytes 8000000 | tf_op jit(solution)/shard_map/pallas_call | solution.py:97
  59.6 5.0 %all-to-all-start = ((f32[8,160,384]{2,1,0:T(8,128)}), f32[8,160,384]{2,1,0:T(8,128)S(1)}, u32[]{:S(2)}, u32[]{:S(2)}) async-start(f32[8,160,384]{2,1,0:T(8,128)} %bitcast.2), calls=%async_computation | async-start | bytes 3932160 | tf_op jit(solution)/shard_map/all_to_all | solution.py:120
  64.7 0.0 copy-start.1
  64.7 24.8 %all-to-all-done = f32[8,160,384]{2,1,0:T(8,128)S(1)} async-done(((f32[8,160,384]{2,1,0:T(8,128)}), f32[8,160,384]{2,1,0:T(8,128)S(1)}, u32[]{:S(2)}, u32[]{:S(2)}) %all-to-all-start) | async-done | bytes 1966112 | tf_op jit(solution)/shard_map/all_to_all | solution.py:120
  89.5 0.8 reduce_sum.18
  90.3 5.9 %all-to-all-start.1 = ((f32[4,40,384]{2,1,0:T(8,128)}), f32[4,40,384]{2,1,0:T(8,128)S(1)}, u32[]{:S(2)}, u32[]{:S(2)}) async-start(f32[4,40,384]{2,1,0:T(8,128)} %bitcast.3), calls=%async_computation.1 | async-start | bytes 491520 | tf_op jit(solution)/shard_map/all_to_all | solution.py:121
  96.2 0.0 copy-done.1
  96.2 0.1 broadcast_compare_fusion.1
  96.3 0.1 broadcast_compare_fusion
  96.4 7.9 %all-to-all-done.1 = f32[4,40,384]{2,1,0:T(8,128)S(1)} async-done(((f32[4,40,384]{2,1,0:T(8,128)}), f32[4,40,384]{2,1,0:T(8,128)S(1)}, u32[]{:S(2)}, u32[]{:S(2)}) %all-to-all-start.1) | async-done | bytes 245792 | tf_op jit(solution)/shard_map/all_to_all | solution.py:121
  104.3 0.7 bitcast_select_fusion
  (4 shorter events, 0.0 us)
Async XLA Ops:
  1.8 53.8 %copy-start.2 = (s32[5]{0:T(128)S(1)}, s32[5]{0:T(128)}, u32[]{:S(2)}) copy-start(s32[5]{0:T(128)} %param.6) | copy-start | bytes 64
  43.8 12.0 %collective-permute-start = (f32[16,5,24,128]{3,2,1,0:T(8,128)S(1)}, f32[16,5,24,128]{3,2,1,0:T(8,128)S(1)}, u32[]{:S(2)}, u32[]{:S(2)}) collective-permute-start(f32[16,5,24,128]{3,2,1,0:T(8,128)S(1)} %bitcast.6), channel_id=1, source_target_pairs={{0,1},{1,0},{2,3},{3,2},{4,5},{5,4},{6,7},{7,6},{8,9},{9,8},{10,11... | collective-permute-start | bytes 2949128 | tf_op jit(solution)/shard_map/ppermute | solution.py:117
  53.3 1.8 %copy-start = (f32[5,384,384]{2,1,0:T(8,128)S(1)}, f32[5,384,384]{2,1,0:T(8,128)}, u32[]{:S(2)}) copy-start(f32[5,384,384]{2,1,0:T(8,128)} %integrals_ref.1) | copy-start | bytes 8847364
  59.6 29.9 %all-to-all-start = ((f32[8,160,384]{2,1,0:T(8,128)}), f32[8,160,384]{2,1,0:T(8,128)S(1)}, u32[]{:S(2)}, u32[]{:S(2)}) async-start(f32[8,160,384]{2,1,0:T(8,128)} %bitcast.2), calls=%async_computation | async-start | bytes 3932160 | tf_op jit(solution)/shard_map/all_to_all | solution.py:120
  64.7 31.5 %copy-start.1 = (s32[5]{0:T(128)S(1)}, s32[5]{0:T(128)}, u32[]{:S(2)}) copy-start(s32[5]{0:T(128)} %param.7) | copy-start | bytes 64
  90.3 14.0 %all-to-all-start.1 = ((f32[4,40,384]{2,1,0:T(8,128)}), f32[4,40,384]{2,1,0:T(8,128)S(1)}, u32[]{:S(2)}, u32[]{:S(2)}) async-start(f32[4,40,384]{2,1,0:T(8,128)} %bitcast.3), calls=%async_computation.1 | async-start | bytes 491520 | tf_op jit(solution)/shard_map/all_to_all | solution.py:121

commit v6 on v4

--- a/solution.py
+++ b/solution.py
@@ -11,9 +11,11 @@
 NX, YH, YL, ZH, ZL, CORES = 4, 4, 2, 4, 4, 2
 BLOCKS, ROWS, PAIRS, COLS = 5, 32, 96, 384
 LANES = 128
+PACKED = ROWS * PAIRS // LANES
 HALF = ZL * ROWS
 FULL = CORES * HALF
 LIMIT = 24 * 1024 * 1024
+COLUMN_LEFT, ROW_LEFT = BLOCKS + 1, 2 * BLOCKS + 1
 
 
 def split(integrals_ref, bhi_ref, blo_ref):
@@ -40,13 +42,38 @@
     )(integrals)
 
 
+def pack(rows_ref, packed_ref):
+    third = LANES - PAIRS
+    rows = rows_ref[...]
+    last = [rows[:, PACKED:, i * third:(i + 1) * third] for i in range(3)]
+    packed_ref[:, :, :PAIRS] = rows[:, :PACKED]
+    packed_ref[:, :, PAIRS:] = jnp.concatenate(last, axis=1)
+
+
+def pack_rows(amplitudes):
+    whole = pl.BlockSpec(memory_space=pltpu.VMEM)
+    return pl.pallas_call(
+        pack,
+        out_shape=jax.ShapeDtypeStruct((BLOCKS, PACKED, LANES), jnp.float32),
+        in_specs=[whole],
+        out_specs=whole,
+        compiler_params=pltpu.CompilerParams(vmem_limit_bytes=LIMIT),
+    )(amplitudes)
+
+
+def unpack(rows):
+    last = [rows[:, i * 8:(i + 1) * 8, PAIRS:] for i in range(3)]
+    return jnp.concatenate([rows[:, :, :PAIRS], jnp.concatenate(last, axis=2)], axis=1)
+
+
 def product(meta_ref, own_ref, other_ref, bhi_ref, blo_ref, out_ref, ahi, alo):
+    core = meta_ref[BLOCKS]
+
     for h in range(ZH):
         pad = slice(h * LANES + PAIRS, (h + 1) * LANES)
         for ref in (ahi, alo):
             ref[:, :, pad] = jnp.zeros((2, FULL, LANES - PAIRS), jnp.bfloat16)
 
-    core = meta_ref[BLOCKS]
     lane = lax.broadcasted_iota(jnp.int32, (HALF, PAIRS), 1)
     dot = functools.partial(jnp.dot, preferred_element_type=jnp.float32)
     for g in range(BLOCKS):
@@ -57,7 +84,7 @@
             at = slice(h * LANES, h * LANES + PAIRS)
             for part, ref in enumerate((own_ref, other_ref)):
                 rows = slice(part * HALF, (part + 1) * HALF)
-                a = ref[h * ZL:(h + 1) * ZL, g].reshape(HALF, PAIRS)
+                a = unpack(ref[h * ZL:(h + 1) * ZL, g]).reshape(HALF, PAIRS)
                 a = jnp.where(keep, a, 0.0)
                 high = a.astype(jnp.bfloat16)
                 ahi[slot, rows, at] = high
@@ -85,21 +112,42 @@
     )(meta, own, other, bhi, blo)
 
 
+def finish(meta_ref, parts_ref, out_ref):
+    row = lax.broadcasted_iota(jnp.int32, (8, COLS), 0)
+    column = lax.broadcasted_iota(jnp.int32, (8, COLS), 1)
+    for g in range(BLOCKS):
+        rows = slice(g * 8, (g + 1) * 8)
+        total = (parts_ref[0, rows] + parts_ref[1, rows]) + (parts_ref[2, rows] + parts_ref[3, rows])
+        used = jnp.logical_and(row < meta_ref[ROW_LEFT + g], column < meta_ref[COLUMN_LEFT + g])
+        out_ref[g] = jnp.where(used, total, 0.0)
+
+
+def final_rows(meta, parts):
+    whole = pl.BlockSpec(memory_space=pltpu.VMEM)
+    return pl.pallas_call(
+        finish,
+        out_shape=jax.ShapeDtypeStruct((BLOCKS, 8, COLS), jnp.float32),
+        in_specs=[pl.BlockSpec(memory_space=pltpu.SMEM), whole],
+        out_specs=whole,
+        compiler_params=pltpu.CompilerParams(vmem_limit_bytes=LIMIT),
+    )(meta, parts)
+
+
 def per_device(amplitudes, integrals, pair_counts, row_counts):
     y = lax.axis_index("yh") * YL + lax.axis_index("yl")
     gx = y * NX + lax.axis_index("x")
     core = lax.axis_index("c")
-    own = lax.all_gather(amplitudes, ("zh", "zl"), axis=0, tiled=False)
+    column_first = ((lax.axis_index("zh") * ZL + lax.axis_index("zl")) * CORES + core) * COLS
+    meta = jnp.concatenate(
+        [pair_counts - gx * COLS, core[None], pair_counts - column_first, row_counts - gx * 8]
+    )
+    own = lax.all_gather(pack_rows(amplitudes), ("zh", "zl"), axis=0, tiled=False)
     other = lax.ppermute(own, "c", [(0, 1), (1, 0)])
-    partial = partial_sums(jnp.append(pair_counts - gx * COLS, core), own, other, integrals)
+    partial = partial_sums(meta, own, other, integrals)
     sent = partial.reshape(YL * NX, YH * BLOCKS * 8, COLS)
     near = lax.all_to_all(sent, ("yl", "x"), 0, 0, tiled=True).sum(0)
-    far = lax.all_to_all(near.reshape(YH, BLOCKS * 8, COLS), "yh", 0, 0, tiled=True).sum(0)
-    column_first = ((lax.axis_index("zh") * ZL + lax.axis_index("zl")) * CORES + core) * COLS
-    column_used = column_first + lax.iota(jnp.int32, COLS)[None, :] < pair_counts[:, None]
-    row_used = gx * 8 + lax.iota(jnp.int32, 8)[None, :] < row_counts[:, None]
-    keep = jnp.logical_and(row_used[:, :, None], column_used[:, None, :])
-    return jnp.where(keep, far.reshape(BLOCKS, 8, COLS), 0.0)
+    far = lax.all_to_all(near.reshape(YH, BLOCKS * 8, COLS), "yh", 0, 0, tiled=True)
+    return final_rows(meta, far)
 
 
 def solution(mesh):

time: 108 us -> 105 us (0.972)
  blocking collectives: 44.4 us -> 85.5 us
  waiting for transfers between devices: 32.8 us -> 0.01 us
  starting transfers between devices: 20.7 us -> 9.49 us
  other arithmetic: 1.75 us -> 0.2 us
    all_to_all x0 -> x2, blocking collectives: none -> 43.5 us  [the longest x1 29.5 us: per_device(): near = lax.all_to_all(sent, ('yl', 'x'), 0, 0, tiled=True).sum(0)]
    all_to_all x2 -> x0, waiting for transfers between devices: 32.7 us -> none  [the longest x1 24.8 us: per_device(): near = lax.all_to_all(sent, ('yl', 'x'), 0, 0, tiled=True).sum(0)]
    all_to_all x2 -> x0, starting transfers between devices: 10.9 us -> none  [the longest x1 5.92 us: per_device(): lax.all_to_all(near.reshape(YH, BLOCKS * 8, COLS), 'yh', 0, 0, tiled=True)]
    all_gather x1, blocking collectives: 44.4 us -> 42.1 us  [per_device(): lax.all_gather(pack_rows(amplitudes), ('zh', 'zl'), axis=0, tiled=False)]
    pallas_call x1, Pallas kernels: 4.51 us -> 3.04 us  [partial_sums(): pl.pallas_call(product, out_shape=jax.ShapeDtypeStruct((YL, NX, YH, BLOCK...]
    pallas_call x0 -> x2, Pallas kernels: none -> 1.33 us  [the longest x1 1.18 us: final_rows(): pl.pallas_call(finish, out_shape=jax.ShapeDtypeStruct((BLOCKS, 8, COLS),...]
    unnamed x6 -> x8, local copies, waits for them, and re-layouts: 1.84 us -> 2.72 us
  transfers between devices with their start and end apart: 3 -> 1, of which waited for: 3 -> 0; matrix products, arithmetic and copies ran while one was open for 0% -> 0% of each run, Pallas kernels for 0% -> 1%
where the time goes in v6:
time: 105 us; the launch traced here: 103 us
  blocking collectives  85.5 us (81%)
  starting transfers between devices  9.49 us (9%)
  Pallas kernels  4.88 us (5%)
  local copies, waits for them, and re-layouts  2.72 us (3%)
    all_gather x1, blocking collectives, per_device(): lax.all_gather(pack_rows(amplitudes), ('zh', 'zl'), axis=0, tiled=False)  42.1 us
    all_to_all x1, blocking collectives, per_device(): near = lax.all_to_all(sent, ('yl', 'x'), 0, 0, tiled=True).sum(0)  29.5 us
    all_to_all x1, blocking collectives, per_device(): lax.all_to_all(near.reshape(YH, BLOCKS * 8, COLS), 'yh', 0, 0, tiled=True)  13.9 us
    ppermute x1, starting transfers between devices, per_device(): other = lax.ppermute(own, 'c', [(0, 1), (1, 0)])  9.49 us
    pallas_call x1, Pallas kernels, partial_sums(): pl.pallas_call(product, out_shape=jax.ShapeDtypeStruct((YL, NX, YH, BLOCK...  3.04 us
    unnamed x8, local copies, waits for them, and re-layouts  2.72 us
  transfers between devices with their start and end apart: 1, of which 0 were waited for; matrix products, arithmetic and copies ran while one was open for 0% of the time, Pallas kernels for 1%

profile of v6, /device:TPU:1, one launch (start us, length us, event | category | flops | bytes accessed | tf_op | source)
XLA Modules:
  0.0 102.9 jit_solution(16513395401057176109)
XLA Ops:
  0.0 0.0 copy-start.1
  0.0 0.9 copy-done.1
  0.9 0.1 shard_map.46
  1.0 0.0 copy-start.3
  1.0 0.0 copy-start.2
  1.0 42.1 %all-gather = f32[80,24,128]{2,1,0:T(8,128)S(1)} all-gather(f32[5,24,128]{2,1,0:T(8,128)S(1)} %shard_map.46), channel_id=2, replica_groups=mesh['yh'=4,'yl'=2,'x'=4,'zh'=4,'zl'=4,'c'=2] {'zh','zl'}, dimensions={0}, use_global_device_ids=true | all-gather | bytes 1044480 | tf_op jit(solution)/shard_map/all_gather | solution.py:144
  43.1 9.5 %collective-permute-start = (f32[16,5,24,128]{3,2,1,0:T(8,128)S(1)}, f32[16,5,24,128]{3,2,1,0:T(8,128)S(1)}, u32[]{:S(2)}, u32[]{:S(2)}) collective-permute-start(f32[16,5,24,128]{3,2,1,0:T(8,128)S(1)} %bitcast.5), channel_id=1, source_target_pairs={{0,1},{1,0},{2,3},{3,2},{4,5},{5,4},{6,7},{7,6},{8,9},{9,8},{10,11... | collective-permute-start | bytes 2949128 | tf_op jit(solution)/shard_map/ppermute | solution.py:145
  52.6 0.0 copy-start
  52.6 1.8 %copy-done = f32[5,384,384]{2,1,0:T(8,128)S(1)} copy-done((f32[5,384,384]{2,1,0:T(8,128)S(1)}, f32[5,384,384]{2,1,0:T(8,128)}, u32[]{:S(2)}) %copy-start) | copy-done | bytes 2949144
  54.4 0.5 shard_map.47
  55.0 0.0 copy-done.3
  55.0 0.0 copy-done.2
  55.0 0.1 pad_add_fusion.meta_ref
  55.1 0.0 collective-permute-done.other_ref
  55.1 3.0 %shard_map.48 = f32[2,4,4,5,8,384]{5,4,3,2,1,0:T(8,128)S(1)} custom-call(s32[16]{0:T(128)S(1)} %pad_add_fusion.meta_ref, f32[16,5,24,128]{3,2,1,0:T(8,128)S(1)} %bitcast.6, f32[16,5,24,128]{3,2,1,0:T(8,128)S(1)} %collective-permute-done.other_ref, bf16[5,512,384]{2,1,0:T(8,128)(2,1)S(1)} %get-tuple-element.7.bhi_ref, ...), custom_call_target="tpu_custom_call" | custom-call | flops 1200000000 | bytes 8000000 | tf_op jit(solution)/shard_map/pallas_call | solution.py:104
  58.1 29.5 %all_to_all.10 = f32[8,160,384]{2,1,0:T(8,128)S(1)} all-to-all(f32[8,160,384]{2,1,0:T(8,128)S(1)} %bitcast.4), channel_id=1, replica_groups=mesh['yh'=4,'yl'=2,'x'=4,'zh'=4,'zl'=4,'c'=2] {'yl','x'}, dimensions={0} | all-to-all | bytes 3932160 | tf_op jit(solution)/shard_map/all_to_all | solution.py:148
  87.7 0.1 reduce_sum.9
  87.8 13.9 %all_to_all.11.parts_ref = f32[4,40,384]{2,1,0:T(8,128)S(1)} all-to-all(f32[4,40,384]{2,1,0:T(8,128)S(1)} %bitcast.7), channel_id=1, replica_groups=mesh['yh'=4,'yl'=2,'x'=4,'zh'=4,'zl'=4,'c'=2] {'yh'}, dimensions={0} | all-to-all | bytes 491520 | tf_op jit(solution)/shard_map/all_to_all | solution.py:149
  101.7 1.2 %shard_map.49 = f32[5,8,384]{2,1,0:T(8,128)} custom-call(s32[16]{0:T(128)S(1)} %pad_add_fusion.meta_ref, f32[4,40,384]{2,1,0:T(8,128)S(1)} %all_to_all.11.parts_ref), custom_call_target="tpu_custom_call" | custom-call | tf_op jit(solution)/shard_map/pallas_call | solution.py:127
  (2 shorter events, 0.0 us)
Async XLA Ops:
  0.0 0.9 copy-start.1
  1.0 53.9 %copy-start.3 = (s32[5]{0:T(128)S(1)}, s32[5]{0:T(128)}, u32[]{:S(2)}) copy-start(s32[5]{0:T(128)} %param.7) | copy-start | bytes 64
  1.0 54.0 %copy-start.2 = (s32[5]{0:T(128)S(1)}, s32[5]{0:T(128)}, u32[]{:S(2)}) copy-start(s32[5]{0:T(128)} %param.6) | copy-start | bytes 64
  43.1 12.0 %collective-permute-start = (f32[16,5,24,128]{3,2,1,0:T(8,128)S(1)}, f32[16,5,24,128]{3,2,1,0:T(8,128)S(1)}, u32[]{:S(2)}, u32[]{:S(2)}) collective-permute-start(f32[16,5,24,128]{3,2,1,0:T(8,128)S(1)} %bitcast.5), channel_id=1, source_target_pairs={{0,1},{1,0},{2,3},{3,2},{4,5},{5,4},{6,7},{7,6},{8,9},{9,8},{10,11... | collective-permute-start | bytes 2949128 | tf_op jit(solution)/shard_map/ppermute | solution.py:145
  52.6 1.8 %copy-start = (f32[5,384,384]{2,1,0:T(8,128)S(1)}, f32[5,384,384]{2,1,0:T(8,128)}, u32[]{:S(2)}) copy-start(f32[5,384,384]{2,1,0:T(8,128)} %integrals_ref.1) | copy-start | bytes 8847364

commit v7 on v6

--- a/solution.py
+++ b/solution.py
@@ -67,8 +67,7 @@
 
 
 def product(meta_ref, own_ref, other_ref, bhi_ref, blo_ref, out_ref, ahi, alo):
-    core = meta_ref[BLOCKS]
-
+    group = meta_ref[BLOCKS]
     for h in range(ZH):
         pad = slice(h * LANES + PAIRS, (h + 1) * LANES)
         for ref in (ahi, alo):
@@ -91,8 +90,8 @@
                 alo[slot, rows, at] = (a - high.astype(jnp.float32)).astype(jnp.bfloat16)
         total = dot(ahi[slot], bhi_ref[g]) + (dot(ahi[slot], blo_ref[g]) + dot(alo[slot], bhi_ref[g]))
         for part in range(CORES):
-            side = core if part == 0 else 1 - core
             for l in range(ZL):
+                side = group if (l + part) % 2 == 0 else 1 - group
                 for x in range(NX):
                     first = part * HALF + l * ROWS + x * 8
                     out_ref[side, x, l, g] = total[first:first + 8]
@@ -137,11 +136,13 @@
     y = lax.axis_index("yh") * YL + lax.axis_index("yl")
     gx = y * NX + lax.axis_index("x")
     core = lax.axis_index("c")
+    group = lax.rem(core + lax.axis_index("zl"), CORES)
     column_first = ((lax.axis_index("zh") * ZL + lax.axis_index("zl")) * CORES + core) * COLS
     meta = jnp.concatenate(
-        [pair_counts - gx * COLS, core[None], pair_counts - column_first, row_counts - gx * 8]
+        [pair_counts - gx * COLS, group[None], pair_counts - column_first, row_counts - gx * 8]
     )
-    own = lax.all_gather(pack_rows(amplitudes), ("zh", "zl"), axis=0, tiled=False)
+    rings = [[z * CORES + (q + z) % CORES for z in range(ZH * ZL)] for q in range(CORES)]
+    own = lax.all_gather(pack_rows(amplitudes), ("zh", "zl", "c"), axis_index_groups=rings)
     other = lax.ppermute(own, "c", [(0, 1), (1, 0)])
     partial = partial_sums(meta, own, other, integrals)
     sent = partial.reshape(YL * NX, YH * BLOCKS * 8, COLS)

time: 105 us -> 103 us (0.981)
  starting transfers between devices: 9.49 us -> 2.07 us
  blocking collectives: 85.5 us -> 90.8 us
    ppermute x1, starting transfers between devices: 9.49 us -> 2.07 us  [per_device(): other = lax.ppermute(own, 'c', [(0, 1), (1, 0)])]
    all_gather x1, blocking collectives: 42.1 us -> 47.4 us  [per_device(): lax.all_gather(pack_rows(amplitudes), ('zh', 'zl', 'c'), axis_index_group...]
where the time goes in v7:
time: 103 us; the launch traced here: 101 us
  blocking collectives  90.8 us (88%)
  Pallas kernels  4.88 us (5%)
  local copies, waits for them, and re-layouts  2.72 us (3%)
  starting transfers between devices  2.07 us (2%)
    all_gather x1, blocking collectives, per_device(): lax.all_gather(pack_rows(amplitudes), ('zh', 'zl', 'c'), axis_index_group...  47.4 us
    all_to_all x1, blocking collectives, per_device(): near = lax.all_to_all(sent, ('yl', 'x'), 0, 0, tiled=True).sum(0)  29.5 us
    all_to_all x1, blocking collectives, per_device(): lax.all_to_all(near.reshape(YH, BLOCKS * 8, COLS), 'yh', 0, 0, tiled=True)  13.9 us
    pallas_call x1, Pallas kernels, partial_sums(): pl.pallas_call(product, out_shape=jax.ShapeDtypeStruct((YL, NX, YH, BLOCK...  3.04 us
    unnamed x8, local copies, waits for them, and re-layouts  2.72 us
    ppermute x1, starting transfers between devices, per_device(): other = lax.ppermute(own, 'c', [(0, 1), (1, 0)])  2.07 us
  transfers between devices with their start and end apart: 1, of which 0 were waited for; matrix products, arithmetic and copies ran while one was open for 0% of the time, Pallas kernels for 1%

profile of v7, /device:TPU:1, one launch (start us, length us, event | category | flops | bytes accessed | tf_op | source)
XLA Modules:
  0.0 100.7 jit_solution(7483413228391492764)
XLA Ops:
  0.0 0.0 copy-start.1
  0.0 0.9 copy-done.1
  0.9 0.1 shard_map.46
  1.0 0.0 copy-start.3
  1.0 0.0 copy-start.2
  1.0 47.4 %all-gather = f32[80,24,128]{2,1,0:T(8,128)S(1)} all-gather(f32[5,24,128]{2,1,0:T(8,128)S(1)} %shard_map.46), channel_id=2, replica_groups={{0,3,4,7,8,11,12,15,16,19,20,23,24,27,28,31},{1,2,5,6,9,10,13,14,17,18,..., dimensions={0}, use_global_device_ids=true | all-gather | bytes 1044480 | tf_op jit(solution)/shard_map/all_gather | solution.py:145
  48.4 2.1 %collective-permute-start = (f32[16,5,24,128]{3,2,1,0:T(8,128)S(1)}, f32[16,5,24,128]{3,2,1,0:T(8,128)S(1)}, u32[]{:S(2)}, u32[]{:S(2)}) collective-permute-start(f32[16,5,24,128]{3,2,1,0:T(8,128)S(1)} %bitcast.5), channel_id=1, source_target_pairs={{0,1},{1,0},{2,3},{3,2},{4,5},{5,4},{6,7},{7,6},{8,9},{9,8},{10,11... | collective-permute-start | bytes 2949128 | tf_op jit(solution)/shard_map/ppermute | solution.py:146
  50.5 0.0 copy-start
  50.6 1.8 %copy-done = f32[5,384,384]{2,1,0:T(8,128)S(1)} copy-done((f32[5,384,384]{2,1,0:T(8,128)S(1)}, f32[5,384,384]{2,1,0:T(8,128)}, u32[]{:S(2)}) %copy-start) | copy-done | bytes 2949144
  52.4 0.5 shard_map.47
  52.9 0.0 copy-done.3
  52.9 0.0 copy-done.2
  53.0 0.1 pad_add_fusion.meta_ref
  53.0 0.0 collective-permute-done.other_ref
  53.0 3.0 %shard_map.48 = f32[2,4,4,5,8,384]{5,4,3,2,1,0:T(8,128)S(1)} custom-call(s32[16]{0:T(128)S(1)} %pad_add_fusion.meta_ref, f32[16,5,24,128]{3,2,1,0:T(8,128)S(1)} %bitcast.6, f32[16,5,24,128]{3,2,1,0:T(8,128)S(1)} %collective-permute-done.other_ref, bf16[5,512,384]{2,1,0:T(8,128)(2,1)S(1)} %get-tuple-element.7.bhi_ref, ...), custom_call_target="tpu_custom_call" | custom-call | flops 1200000000 | bytes 8000000 | tf_op jit(solution)/shard_map/pallas_call | solution.py:103
  56.1 29.5 %all_to_all.10 = f32[8,160,384]{2,1,0:T(8,128)S(1)} all-to-all(f32[8,160,384]{2,1,0:T(8,128)S(1)} %bitcast.4), channel_id=1, replica_groups=mesh['yh'=4,'yl'=2,'x'=4,'zh'=4,'zl'=4,'c'=2] {'yl','x'}, dimensions={0} | all-to-all | bytes 3932160 | tf_op jit(solution)/shard_map/all_to_all | solution.py:149
  85.6 0.1 reduce_sum.9
  85.7 13.9 %all_to_all.11.parts_ref = f32[4,40,384]{2,1,0:T(8,128)S(1)} all-to-all(f32[4,40,384]{2,1,0:T(8,128)S(1)} %bitcast.7), channel_id=1, replica_groups=mesh['yh'=4,'yl'=2,'x'=4,'zh'=4,'zl'=4,'c'=2] {'yh'}, dimensions={0} | all-to-all | bytes 491520 | tf_op jit(solution)/shard_map/all_to_all | solution.py:150
  99.6 1.2 %shard_map.49 = f32[5,8,384]{2,1,0:T(8,128)} custom-call(s32[16]{0:T(128)S(1)} %pad_add_fusion.meta_ref, f32[4,40,384]{2,1,0:T(8,128)S(1)} %all_to_all.11.parts_ref), custom_call_target="tpu_custom_call" | custom-call | tf_op jit(solution)/shard_map/pallas_call | solution.py:126
  (2 shorter events, 0.0 us)
Async XLA Ops:
  0.0 0.9 copy-start.1
  1.0 51.9 %copy-start.3 = (s32[5]{0:T(128)S(1)}, s32[5]{0:T(128)}, u32[]{:S(2)}) copy-start(s32[5]{0:T(128)} %param.7) | copy-start | bytes 64
  1.0 51.9 %copy-start.2 = (s32[5]{0:T(128)S(1)}, s32[5]{0:T(128)}, u32[]{:S(2)}) copy-start(s32[5]{0:T(128)} %param.6) | copy-start | bytes 64
  48.4 4.6 %collective-permute-start = (f32[16,5,24,128]{3,2,1,0:T(8,128)S(1)}, f32[16,5,24,128]{3,2,1,0:T(8,128)S(1)}, u32[]{:S(2)}, u32[]{:S(2)}) collective-permute-start(f32[16,5,24,128]{3,2,1,0:T(8,128)S(1)} %bitcast.5), channel_id=1, source_target_pairs={{0,1},{1,0},{2,3},{3,2},{4,5},{5,4},{6,7},{7,6},{8,9},{9,8},{10,11... | collective-permute-start | bytes 2949128 | tf_op jit(solution)/shard_map/ppermute | solution.py:146
  50.5 1.8 %copy-start = (f32[5,384,384]{2,1,0:T(8,128)S(1)}, f32[5,384,384]{2,1,0:T(8,128)}, u32[]{:S(2)}) copy-start(f32[5,384,384]{2,1,0:T(8,128)} %integrals_ref.1) | copy-start | bytes 8847364

commit v8 on v7

--- a/solution.py
+++ b/solution.py
@@ -62,8 +62,8 @@
 
 
 def unpack(rows):
-    last = [rows[:, i * 8:(i + 1) * 8, PAIRS:] for i in range(3)]
-    return jnp.concatenate([rows[:, :, :PAIRS], jnp.concatenate(last, axis=2)], axis=1)
+    last = [rows[i * 8:(i + 1) * 8, PAIRS:] for i in range(3)]
+    return jnp.concatenate([rows[:, :PAIRS], jnp.concatenate(last, axis=1)], axis=0)
 
 
 def product(meta_ref, own_ref, other_ref, bhi_ref, blo_ref, out_ref, ahi, alo):
@@ -73,7 +73,7 @@
         for ref in (ahi, alo):
             ref[:, :, pad] = jnp.zeros((2, FULL, LANES - PAIRS), jnp.bfloat16)
 
-    lane = lax.broadcasted_iota(jnp.int32, (HALF, PAIRS), 1)
+    lane = lax.broadcasted_iota(jnp.int32, (ROWS, PAIRS), 1)
     dot = functools.partial(jnp.dot, preferred_element_type=jnp.float32)
     for g in range(BLOCKS):
         slot = g % 2
@@ -81,13 +81,16 @@
         for h in range(ZH):
             keep = lane < left - h * PAIRS
             at = slice(h * LANES, h * LANES + PAIRS)
-            for part, ref in enumerate((own_ref, other_ref)):
-                rows = slice(part * HALF, (part + 1) * HALF)
-                a = unpack(ref[h * ZL:(h + 1) * ZL, g]).reshape(HALF, PAIRS)
-                a = jnp.where(keep, a, 0.0)
-                high = a.astype(jnp.bfloat16)
-                ahi[slot, rows, at] = high
-                alo[slot, rows, at] = (a - high.astype(jnp.float32)).astype(jnp.bfloat16)
+            for l in range(ZL):
+                z = h * ZL + l
+                for part, ref in enumerate((own_ref, other_ref)):
+                    down = group if part == 0 else 1 - group
+                    a = unpack(ref[z + down * (ZH * ZL - 1 - 2 * z), g])
+                    a = jnp.where(keep, a, 0.0)
+                    high = a.astype(jnp.bfloat16)
+                    rows = slice(part * HALF + l * ROWS, part * HALF + (l + 1) * ROWS)
+                    ahi[slot, rows, at] = high
+                    alo[slot, rows, at] = (a - high.astype(jnp.float32)).astype(jnp.bfloat16)
         total = dot(ahi[slot], bhi_ref[g]) + (dot(ahi[slot], blo_ref[g]) + dot(alo[slot], bhi_ref[g]))
         for part in range(CORES):
             for l in range(ZL):
@@ -141,7 +144,8 @@
     meta = jnp.concatenate(
         [pair_counts - gx * COLS, group[None], pair_counts - column_first, row_counts - gx * 8]
     )
-    rings = [[z * CORES + (q + z) % CORES for z in range(ZH * ZL)] for q in range(CORES)]
+    up = [z * CORES + z % CORES for z in range(ZH * ZL)]
+    rings = [up, [device ^ 1 for device in reversed(up)]]
     own = lax.all_gather(pack_rows(amplitudes), ("zh", "zl", "c"), axis_index_groups=rings)
     other = lax.ppermute(own, "c", [(0, 1), (1, 0)])
     partial = partial_sums(meta, own, other, integrals)

time: 103 us -> 102 us (level)
  no operation moved by 1% of the time
where the time goes in v8:
time: 102 us; the launch traced here: 101 us
  blocking collectives  89.9 us (88%)
  Pallas kernels  4.91 us (5%)
  starting transfers between devices  2.93 us (3%)
  local copies, waits for them, and re-layouts  2.72 us (3%)
    all_gather x1, blocking collectives, per_device(): lax.all_gather(pack_rows(amplitudes), ('zh', 'zl', 'c'), axis_index_group...  46.4 us
    all_to_all x1, blocking collectives, per_device(): near = lax.all_to_all(sent, ('yl', 'x'), 0, 0, tiled=True).sum(0)  29.6 us
    all_to_all x1, blocking collectives, per_device(): lax.all_to_all(near.reshape(YH, BLOCKS * 8, COLS), 'yh', 0, 0, tiled=True)  13.9 us
    pallas_call x1, Pallas kernels, partial_sums(): pl.pallas_call(product, out_shape=jax.ShapeDtypeStruct((YL, NX, YH, BLOCK...  3.07 us
    ppermute x1, starting transfers between devices, per_device(): other = lax.ppermute(own, 'c', [(0, 1), (1, 0)])  2.93 us
    unnamed x8, local copies, waits for them, and re-layouts  2.72 us
  transfers between devices with their start and end apart: 1, of which 0 were waited for; matrix products, arithmetic and copies ran while one was open for 0% of the time, Pallas kernels for 1%

profile of v8, /device:TPU:1, one launch (start us, length us, event | category | flops | bytes accessed | tf_op | source)
XLA Modules:
  0.0 100.8 jit_solution(5323343822100630521)
XLA Ops:
  0.0 0.0 copy-start.1
  0.0 0.9 copy-done.1
  0.9 0.1 shard_map.46
  1.0 0.0 copy-start.3
  1.0 0.0 copy-start.2
  1.0 46.4 %all-gather = f32[80,24,128]{2,1,0:T(8,128)S(1)} all-gather(f32[5,24,128]{2,1,0:T(8,128)S(1)} %shard_map.46), channel_id=2, replica_groups={{0,3,4,7,8,11,12,15,16,19,20,23,24,27,28,31},{30,29,26,25,22,21,18,17,1..., dimensions={0}, use_global_device_ids=true | all-gather | bytes 1044480 | tf_op jit(solution)/shard_map/all_gather | solution.py:149
  47.5 2.9 %collective-permute-start = (f32[16,5,24,128]{3,2,1,0:T(8,128)S(1)}, f32[16,5,24,128]{3,2,1,0:T(8,128)S(1)}, u32[]{:S(2)}, u32[]{:S(2)}) collective-permute-start(f32[16,5,24,128]{3,2,1,0:T(8,128)S(1)} %bitcast.5), channel_id=1, source_target_pairs={{0,1},{1,0},{2,3},{3,2},{4,5},{5,4},{6,7},{7,6},{8,9},{9,8},{10,11... | collective-permute-start | bytes 2949128 | tf_op jit(solution)/shard_map/ppermute | solution.py:150
  50.4 0.0 copy-start
  50.4 1.8 %copy-done = f32[5,384,384]{2,1,0:T(8,128)S(1)} copy-done((f32[5,384,384]{2,1,0:T(8,128)S(1)}, f32[5,384,384]{2,1,0:T(8,128)}, u32[]{:S(2)}) %copy-start) | copy-done | bytes 2949144
  52.2 0.5 shard_map.47
  52.8 0.0 copy-done.3
  52.8 0.0 copy-done.2
  52.8 0.1 pad_add_fusion.meta_ref
  52.9 0.0 collective-permute-done.other_ref
  52.9 3.1 %shard_map.48 = f32[2,4,4,5,8,384]{5,4,3,2,1,0:T(8,128)S(1)} custom-call(s32[16]{0:T(128)S(1)} %pad_add_fusion.meta_ref, f32[16,5,24,128]{3,2,1,0:T(8,128)S(1)} %bitcast.6, f32[16,5,24,128]{3,2,1,0:T(8,128)S(1)} %collective-permute-done.other_ref, bf16[5,512,384]{2,1,0:T(8,128)(2,1)S(1)} %get-tuple-element.7.bhi_ref, ...), custom_call_target="tpu_custom_call" | custom-call | flops 1200000000 | bytes 8000000 | tf_op jit(solution)/shard_map/pallas_call | solution.py:106
  56.0 29.6 %all_to_all.10 = f32[8,160,384]{2,1,0:T(8,128)S(1)} all-to-all(f32[8,160,384]{2,1,0:T(8,128)S(1)} %bitcast.4), channel_id=1, replica_groups=mesh['yh'=4,'yl'=2,'x'=4,'zh'=4,'zl'=4,'c'=2] {'yl','x'}, dimensions={0} | all-to-all | bytes 3932160 | tf_op jit(solution)/shard_map/all_to_all | solution.py:153
  85.5 0.1 reduce_sum.9
  85.6 13.9 %all_to_all.11.parts_ref = f32[4,40,384]{2,1,0:T(8,128)S(1)} all-to-all(f32[4,40,384]{2,1,0:T(8,128)S(1)} %bitcast.7), channel_id=1, replica_groups=mesh['yh'=4,'yl'=2,'x'=4,'zh'=4,'zl'=4,'c'=2] {'yh'}, dimensions={0} | all-to-all | bytes 491520 | tf_op jit(solution)/shard_map/all_to_all | solution.py:154
  99.6 1.2 %shard_map.49 = f32[5,8,384]{2,1,0:T(8,128)} custom-call(s32[16]{0:T(128)S(1)} %pad_add_fusion.meta_ref, f32[4,40,384]{2,1,0:T(8,128)S(1)} %all_to_all.11.parts_ref), custom_call_target="tpu_custom_call" | custom-call | tf_op jit(solution)/shard_map/pallas_call | solution.py:129
  (2 shorter events, 0.0 us)
Async XLA Ops:
  0.0 0.9 copy-start.1
  1.0 51.7 %copy-start.3 = (s32[5]{0:T(128)S(1)}, s32[5]{0:T(128)}, u32[]{:S(2)}) copy-start(s32[5]{0:T(128)} %param.7) | copy-start | bytes 64
  1.0 51.8 %copy-start.2 = (s32[5]{0:T(128)S(1)}, s32[5]{0:T(128)}, u32[]{:S(2)}) copy-start(s32[5]{0:T(128)} %param.6) | copy-start | bytes 64
  47.5 5.4 %collective-permute-start = (f32[16,5,24,128]{3,2,1,0:T(8,128)S(1)}, f32[16,5,24,128]{3,2,1,0:T(8,128)S(1)}, u32[]{:S(2)}, u32[]{:S(2)}) collective-permute-start(f32[16,5,24,128]{3,2,1,0:T(8,128)S(1)} %bitcast.5), channel_id=1, source_target_pairs={{0,1},{1,0},{2,3},{3,2},{4,5},{5,4},{6,7},{7,6},{8,9},{9,8},{10,11... | collective-permute-start | bytes 2949128 | tf_op jit(solution)/shard_map/ppermute | solution.py:150
  50.4 1.8 %copy-start = (f32[5,384,384]{2,1,0:T(8,128)S(1)}, f32[5,384,384]{2,1,0:T(8,128)}, u32[]{:S(2)}) copy-start(f32[5,384,384]{2,1,0:T(8,128)} %integrals_ref.1) | copy-start | bytes 8847364

commit v9 on v8

--- a/solution.py
+++ b/solution.py
@@ -37,7 +37,7 @@
         grid=(BLOCKS,),
         in_specs=[pl.BlockSpec((1, COLS, COLS), lambda g: (g, 0, 0))],
         out_specs=[halves, halves],
-        compiler_params=pltpu.CompilerParams(vmem_limit_bytes=LIMIT),
+        compiler_params=pltpu.CompilerParams(vmem_limit_bytes=51000000),
         cost_estimate=pl.CostEstimate(flops=5_000_000, bytes_accessed=7_000_000, transcendentals=0),
     )(integrals)
 

time: 102 us -> 104 us (1.020)
  Pallas kernels: 4.91 us -> 7.88 us
  local copies, waits for them, and re-layouts: 2.72 us -> 0.9 us
    pallas_call x1, Pallas kernels: 0.52 us -> 3.56 us  [split_integrals(): pl.pallas_call(split, out_shape=[jax.ShapeDtypeStruct((BLOCKS, ZH * LANES...]
    unnamed x8 -> x6, local copies, waits for them, and re-layouts: 2.72 us -> 0.9 us
  transfers between devices with their start and end apart: 1 -> 1, of which waited for: 0 -> 0; matrix products, arithmetic and copies ran while one was open for 0% -> 0% of each run, Pallas kernels for 1% -> 3%
where the time goes in v9:
time: 104 us; the launch traced here: 102 us
  blocking collectives  89.9 us (86%)
  Pallas kernels  7.88 us (8%)
  starting transfers between devices  2.93 us (3%)
    all_gather x1, blocking collectives, per_device(): lax.all_gather(pack_rows(amplitudes), ('zh', 'zl', 'c'), axis_index_group...  46.4 us
    all_to_all x1, blocking collectives, per_device(): near = lax.all_to_all(sent, ('yl', 'x'), 0, 0, tiled=True).sum(0)  29.6 us
    all_to_all x1, blocking collectives, per_device(): lax.all_to_all(near.reshape(YH, BLOCKS * 8, COLS), 'yh', 0, 0, tiled=True)  13.9 us
    pallas_call x1, Pallas kernels, split_integrals(): pl.pallas_call(split, out_shape=[jax.ShapeDtypeStruct((BLOCKS, ZH * LANES...  3.56 us
    pallas_call x1, Pallas kernels, partial_sums(): pl.pallas_call(product, out_shape=jax.ShapeDtypeStruct((YL, NX, YH, BLOCK...  3 us
    ppermute x1, starting transfers between devices, per_device(): other = lax.ppermute(own, 'c', [(0, 1), (1, 0)])  2.93 us
  transfers between devices with their start and end apart: 1, of which 0 were waited for; matrix products, arithmetic and copies ran while one was open for 0% of the time, Pallas kernels for 3%

profile of v9, /device:TPU:1, one launch (start us, length us, event | category | flops | bytes accessed | tf_op | source)
XLA Modules:
  0.0 101.9 jit_solution(13307481788494950458)
XLA Ops:
  0.0 0.0 copy-start
  0.0 0.9 copy-done
  0.9 0.1 shard_map.46
  1.0 0.0 copy-start.2
  1.0 0.0 copy-start.1
  1.0 46.4 %all-gather = f32[80,24,128]{2,1,0:T(8,128)S(1)} all-gather(f32[5,24,128]{2,1,0:T(8,128)S(1)} %shard_map.46), channel_id=2, replica_groups={{0,3,4,7,8,11,12,15,16,19,20,23,24,27,28,31},{30,29,26,25,22,21,18,17,1..., dimensions={0}, use_global_device_ids=true | all-gather | bytes 1044480 | tf_op jit(solution)/shard_map/all_gather | solution.py:149
  47.5 2.9 %collective-permute-start = (f32[16,5,24,128]{3,2,1,0:T(8,128)S(1)}, f32[16,5,24,128]{3,2,1,0:T(8,128)S(1)}, u32[]{:S(2)}, u32[]{:S(2)}) collective-permute-start(f32[16,5,24,128]{3,2,1,0:T(8,128)S(1)} %bitcast.5), channel_id=1, source_target_pairs={{0,1},{1,0},{2,3},{3,2},{4,5},{5,4},{6,7},{7,6},{8,9},{9,8},{10,11... | collective-permute-start | bytes 2949128 | tf_op jit(solution)/shard_map/ppermute | solution.py:150
  50.4 3.6 %shard_map.47 = (bf16[5,512,384]{2,1,0:T(8,128)(2,1)S(1)}, bf16[5,512,384]{2,1,0:T(8,128)(2,1)S(1)}) custom-call(f32[5,384,384]{2,1,0:T(8,128)} %integrals_ref.1), custom_call_target="tpu_custom_call" | custom-call | flops 5000000 | bytes 7000000 | tf_op jit(solution)/shard_map/pallas_call | solution.py:34
  54.0 0.0 copy-done.2
  54.0 0.0 copy-done.1
  54.0 0.1 pad_add_fusion.meta_ref
  54.1 0.0 collective-permute-done.other_ref
  54.1 3.0 %shard_map.48 = f32[2,4,4,5,8,384]{5,4,3,2,1,0:T(8,128)S(1)} custom-call(s32[16]{0:T(128)S(1)} %pad_add_fusion.meta_ref, f32[16,5,24,128]{3,2,1,0:T(8,128)S(1)} %bitcast.6, f32[16,5,24,128]{3,2,1,0:T(8,128)S(1)} %collective-permute-done.other_ref, bf16[5,512,384]{2,1,0:T(8,128)(2,1)S(1)} %get-tuple-element.7.bhi_ref, ...), custom_call_target="tpu_custom_call" | custom-call | flops 1200000000 | bytes 8000000 | tf_op jit(solution)/shard_map/pallas_call | solution.py:106
  57.1 29.6 %all_to_all.10 = f32[8,160,384]{2,1,0:T(8,128)S(1)} all-to-all(f32[8,160,384]{2,1,0:T(8,128)S(1)} %bitcast.4), channel_id=1, replica_groups=mesh['yh'=4,'yl'=2,'x'=4,'zh'=4,'zl'=4,'c'=2] {'yl','x'}, dimensions={0} | all-to-all | bytes 3932160 | tf_op jit(solution)/shard_map/all_to_all | solution.py:153
  86.7 0.1 reduce_sum.9
  86.8 13.9 %all_to_all.11.parts_ref = f32[4,40,384]{2,1,0:T(8,128)S(1)} all-to-all(f32[4,40,384]{2,1,0:T(8,128)S(1)} %bitcast.7), channel_id=1, replica_groups=mesh['yh'=4,'yl'=2,'x'=4,'zh'=4,'zl'=4,'c'=2] {'yh'}, dimensions={0} | all-to-all | bytes 491520 | tf_op jit(solution)/shard_map/all_to_all | solution.py:154
  100.7 1.2 %shard_map.49 = f32[5,8,384]{2,1,0:T(8,128)} custom-call(s32[16]{0:T(128)S(1)} %pad_add_fusion.meta_ref, f32[4,40,384]{2,1,0:T(8,128)S(1)} %all_to_all.11.parts_ref), custom_call_target="tpu_custom_call" | custom-call | tf_op jit(solution)/shard_map/pallas_call | solution.py:129
  (2 shorter events, 0.0 us)
Async XLA Ops:
  0.0 0.9 copy-start
  1.0 52.9 %copy-start.2 = (s32[5]{0:T(128)S(1)}, s32[5]{0:T(128)}, u32[]{:S(2)}) copy-start(s32[5]{0:T(128)} %param.7) | copy-start | bytes 64
  1.0 53.0 %copy-start.1 = (s32[5]{0:T(128)S(1)}, s32[5]{0:T(128)}, u32[]{:S(2)}) copy-start(s32[5]{0:T(128)} %param.6) | copy-start | bytes 64
  47.5 6.6 %collective-permute-start = (f32[16,5,24,128]{3,2,1,0:T(8,128)S(1)}, f32[16,5,24,128]{3,2,1,0:T(8,128)S(1)}, u32[]{:S(2)}, u32[]{:S(2)}) collective-permute-start(f32[16,5,24,128]{3,2,1,0:T(8,128)S(1)} %bitcast.5), channel_id=1, source_target_pairs={{0,1},{1,0},{2,3},{3,2},{4,5},{5,4},{6,7},{7,6},{8,9},{9,8},{10,11... | collective-permute-start | bytes 2949128 | tf_op jit(solution)/shard_map/ppermute | solution.py:150

commit v10 on v9

--- a/solution.py
+++ b/solution.py
@@ -18,26 +18,35 @@
 COLUMN_LEFT, ROW_LEFT = BLOCKS + 1, 2 * BLOCKS + 1
 
 
-def split(integrals_ref, bhi_ref, blo_ref):
+def split(integrals_ref, bhi_ref, blo_ref, held, arrived):
+    def fetch(g):
+        return pltpu.make_async_copy(integrals_ref.at[g], held.at[g], arrived.at[g])
+
+    for g in range(BLOCKS):
+        fetch(g).start()
     pad = jnp.zeros((LANES - PAIRS, COLS), jnp.bfloat16)
-    for h in range(ZH):
-        b = integrals_ref[0, h * PAIRS:(h + 1) * PAIRS, :]
-        high = b.astype(jnp.bfloat16)
-        low = (b - high.astype(jnp.float32)).astype(jnp.bfloat16)
-        for ref, value in ((bhi_ref, high), (blo_ref, low)):
-            ref[0, h * LANES:h * LANES + PAIRS, :] = value
-            ref[0, h * LANES + PAIRS:(h + 1) * LANES, :] = pad
+    for g in range(BLOCKS):
+        fetch(g).wait()
+        for h in range(ZH):
+            b = held[g, h * PAIRS:(h + 1) * PAIRS, :]
+            high = b.astype(jnp.bfloat16)
+            low = (b - high.astype(jnp.float32)).astype(jnp.bfloat16)
+            for ref, value in ((bhi_ref, high), (blo_ref, low)):
+                ref[g, h * LANES:h * LANES + PAIRS, :] = value
+                ref[g, h * LANES + PAIRS:(h + 1) * LANES, :] = pad
 
 
 def split_integrals(integrals):
-    halves = pl.BlockSpec((1, ZH * LANES, COLS), lambda g: (g, 0, 0))
+    whole = pl.BlockSpec(memory_space=pltpu.VMEM)
     return pl.pallas_call(
         split,
         out_shape=[jax.ShapeDtypeStruct((BLOCKS, ZH * LANES, COLS), jnp.bfloat16)] * 2,
-        grid=(BLOCKS,),
-        in_specs=[pl.BlockSpec((1, COLS, COLS), lambda g: (g, 0, 0))],
-        out_specs=[halves, halves],
-        compiler_params=pltpu.CompilerParams(vmem_limit_bytes=51000000),
+        in_specs=[pl.BlockSpec(memory_space=pltpu.HBM)],
+        out_specs=[whole, whole],
+        scratch_shapes=[
+            pltpu.VMEM((BLOCKS, COLS, COLS), jnp.float32), pltpu.SemaphoreType.DMA((BLOCKS,))
+        ],
+        compiler_params=pltpu.CompilerParams(vmem_limit_bytes=51_000_000),
         cost_estimate=pl.CostEstimate(flops=5_000_000, bytes_accessed=7_000_000, transcendentals=0),
     )(integrals)
 

time: 104 us -> 102 us (0.981)
  Pallas kernels: 7.88 us -> 6.24 us
    pallas_call x1, Pallas kernels: 3.56 us -> 1.91 us  [split_integrals(): pl.pallas_call(split, out_shape=[jax.ShapeDtypeStruct((BLOCKS, ZH * LANES...]
  transfers between devices with their start and end apart: 1 -> 1, of which waited for: 0 -> 1; matrix products, arithmetic and copies ran while one was open for 0% -> 0% of each run, Pallas kernels for 3% -> 2%
where the time goes in v10:
time: 102 us; the launch traced here: 100 us
  blocking collectives  89.8 us (88%)
  Pallas kernels  6.24 us (6%)
  starting transfers between devices  2.93 us (3%)
    all_gather x1, blocking collectives, per_device(): lax.all_gather(pack_rows(amplitudes), ('zh', 'zl', 'c'), axis_index_group...  46.4 us
    all_to_all x1, blocking collectives, per_device(): near = lax.all_to_all(sent, ('yl', 'x'), 0, 0, tiled=True).sum(0)  29.4 us
    all_to_all x1, blocking collectives, per_device(): lax.all_to_all(near.reshape(YH, BLOCKS * 8, COLS), 'yh', 0, 0, tiled=True)  13.9 us
    pallas_call x1, Pallas kernels, partial_sums(): pl.pallas_call(product, out_shape=jax.ShapeDtypeStruct((YL, NX, YH, BLOCK...  3 us
    ppermute x1, starting transfers between devices, per_device(): other = lax.ppermute(own, 'c', [(0, 1), (1, 0)])  2.93 us
  transfers between devices with their start and end apart: 1, of which 1 were waited for; matrix products, arithmetic and copies ran while one was open for 0% of the time, Pallas kernels for 2%

profile of v10, /device:TPU:1, one launch (start us, length us, event | category | flops | bytes accessed | tf_op | source)
XLA Modules:
  0.0 100.2 jit_solution(18154982032883087762)
XLA Ops:
  0.0 0.0 copy-start
  0.0 0.9 copy-done
  0.9 0.1 shard_map.46
  1.0 0.0 copy-start.2
  1.0 0.0 copy-start.1
  1.0 46.4 %all-gather = f32[80,24,128]{2,1,0:T(8,128)S(1)} all-gather(f32[5,24,128]{2,1,0:T(8,128)S(1)} %shard_map.46), channel_id=2, replica_groups={{0,3,4,7,8,11,12,15,16,19,20,23,24,27,28,31},{30,29,26,25,22,21,18,17,1..., dimensions={0}, use_global_device_ids=true | all-gather | bytes 1044480 | tf_op jit(solution)/shard_map/all_gather | solution.py:158
  47.5 2.9 %collective-permute-start = (f32[16,5,24,128]{3,2,1,0:T(8,128)S(1)}, f32[16,5,24,128]{3,2,1,0:T(8,128)S(1)}, u32[]{:S(2)}, u32[]{:S(2)}) collective-permute-start(f32[16,5,24,128]{3,2,1,0:T(8,128)S(1)} %bitcast.5), channel_id=1, source_target_pairs={{0,1},{1,0},{2,3},{3,2},{4,5},{5,4},{6,7},{7,6},{8,9},{9,8},{10,11... | collective-permute-start | bytes 2949128 | tf_op jit(solution)/shard_map/ppermute | solution.py:159
  50.4 1.9 %shard_map.47 = (bf16[5,512,384]{2,1,0:T(8,128)(2,1)S(1)}, bf16[5,512,384]{2,1,0:T(8,128)(2,1)S(1)}) custom-call(f32[5,384,384]{2,1,0:T(8,128)} %integrals_ref.1), custom_call_target="tpu_custom_call" | custom-call | flops 5000000 | bytes 7000000 | tf_op jit(solution)/shard_map/pallas_call | solution.py:41
  52.3 0.0 copy-done.2
  52.4 0.0 copy-done.1
  52.4 0.1 pad_add_fusion.meta_ref
  52.5 0.1 collective-permute-done.other_ref
  52.6 3.0 %shard_map.48 = f32[2,4,4,5,8,384]{5,4,3,2,1,0:T(8,128)S(1)} custom-call(s32[16]{0:T(128)S(1)} %pad_add_fusion.meta_ref, f32[16,5,24,128]{3,2,1,0:T(8,128)S(1)} %bitcast.6, f32[16,5,24,128]{3,2,1,0:T(8,128)S(1)} %collective-permute-done.other_ref, bf16[5,512,384]{2,1,0:T(8,128)(2,1)S(1)} %get-tuple-element.7.bhi_ref, ...), custom_call_target="tpu_custom_call" | custom-call | flops 1200000000 | bytes 8000000 | tf_op jit(solution)/shard_map/pallas_call | solution.py:115
  55.6 29.4 %all_to_all.10 = f32[8,160,384]{2,1,0:T(8,128)S(1)} all-to-all(f32[8,160,384]{2,1,0:T(8,128)S(1)} %bitcast.4), channel_id=1, replica_groups=mesh['yh'=4,'yl'=2,'x'=4,'zh'=4,'zl'=4,'c'=2] {'yl','x'}, dimensions={0} | all-to-all | bytes 3932160 | tf_op jit(solution)/shard_map/all_to_all | solution.py:162
  85.0 0.1 reduce_sum.9
  85.1 13.9 %all_to_all.11.parts_ref = f32[4,40,384]{2,1,0:T(8,128)S(1)} all-to-all(f32[4,40,384]{2,1,0:T(8,128)S(1)} %bitcast.7), channel_id=1, replica_groups=mesh['yh'=4,'yl'=2,'x'=4,'zh'=4,'zl'=4,'c'=2] {'yh'}, dimensions={0} | all-to-all | bytes 491520 | tf_op jit(solution)/shard_map/all_to_all | solution.py:163
  99.1 1.2 %shard_map.49 = f32[5,8,384]{2,1,0:T(8,128)} custom-call(s32[16]{0:T(128)S(1)} %pad_add_fusion.meta_ref, f32[4,40,384]{2,1,0:T(8,128)S(1)} %all_to_all.11.parts_ref), custom_call_target="tpu_custom_call" | custom-call | tf_op jit(solution)/shard_map/pallas_call | solution.py:138
  (2 shorter events, 0.0 us)
Async XLA Ops:
  0.0 0.9 copy-start
  1.0 51.3 %copy-start.2 = (s32[5]{0:T(128)S(1)}, s32[5]{0:T(128)}, u32[]{:S(2)}) copy-start(s32[5]{0:T(128)} %param.7) | copy-start | bytes 64
  1.0 51.3 %copy-start.1 = (s32[5]{0:T(128)S(1)}, s32[5]{0:T(128)}, u32[]{:S(2)}) copy-start(s32[5]{0:T(128)} %param.6) | copy-start | bytes 64
  47.5 5.1 %collective-permute-start = (f32[16,5,24,128]{3,2,1,0:T(8,128)S(1)}, f32[16,5,24,128]{3,2,1,0:T(8,128)S(1)}, u32[]{:S(2)}, u32[]{:S(2)}) collective-permute-start(f32[16,5,24,128]{3,2,1,0:T(8,128)S(1)} %bitcast.5), channel_id=1, source_target_pairs={{0,1},{1,0},{2,3},{3,2},{4,5},{5,4},{6,7},{7,6},{8,9},{9,8},{10,11... | collective-permute-start | bytes 2949128 | tf_op jit(solution)/shard_map/ppermute | solution.py:159

commit v11 on v10

--- a/solution.py
+++ b/solution.py
@@ -14,6 +14,7 @@
 PACKED = ROWS * PAIRS // LANES
 HALF = ZL * ROWS
 FULL = CORES * HALF
+SLOTS = 1
 LIMIT = 24 * 1024 * 1024
 COLUMN_LEFT, ROW_LEFT = BLOCKS + 1, 2 * BLOCKS + 1
 
@@ -80,12 +81,12 @@
     for h in range(ZH):
         pad = slice(h * LANES + PAIRS, (h + 1) * LANES)
         for ref in (ahi, alo):
-            ref[:, :, pad] = jnp.zeros((2, FULL, LANES - PAIRS), jnp.bfloat16)
+            ref[:, :, pad] = jnp.zeros((SLOTS, FULL, LANES - PAIRS), jnp.bfloat16)
 
     lane = lax.broadcasted_iota(jnp.int32, (ROWS, PAIRS), 1)
     dot = functools.partial(jnp.dot, preferred_element_type=jnp.float32)
     for g in range(BLOCKS):
-        slot = g % 2
+        slot = g % SLOTS
         left = meta_ref[g]
         for h in range(ZH):
             keep = lane < left - h * PAIRS
@@ -117,7 +118,7 @@
         out_shape=jax.ShapeDtypeStruct((YL, NX, YH, BLOCKS, 8, COLS), jnp.float32),
         in_specs=[pl.BlockSpec(memory_space=pltpu.SMEM)] + [whole] * 4,
         out_specs=whole,
-        scratch_shapes=[pltpu.VMEM((2, FULL, ZH * LANES), jnp.bfloat16)] * 2,
+        scratch_shapes=[pltpu.VMEM((SLOTS, FULL, ZH * LANES), jnp.bfloat16)] * 2,
         compiler_params=pltpu.CompilerParams(vmem_limit_bytes=LIMIT),
         cost_estimate=pl.CostEstimate(flops=1_200_000_000, bytes_accessed=8_000_000, transcendentals=0),
     )(meta, own, other, bhi, blo)

time: 102 us -> 102 us (level)
  no operation moved by 1% of the time
where the time goes in v11:
time: 102 us; the launch traced here: 100 us
  blocking collectives  89.8 us (88%)
  Pallas kernels  6.17 us (6%)
  starting transfers between devices  2.93 us (3%)
    all_gather x1, blocking collectives, per_device(): lax.all_gather(pack_rows(amplitudes), ('zh', 'zl', 'c'), axis_index_group...  46.4 us
    all_to_all x1, blocking collectives, per_device(): near = lax.all_to_all(sent, ('yl', 'x'), 0, 0, tiled=True).sum(0)  29.4 us
    all_to_all x1, blocking collectives, per_device(): lax.all_to_all(near.reshape(YH, BLOCKS * 8, COLS), 'yh', 0, 0, tiled=True)  13.9 us
    pallas_call x1, Pallas kernels, partial_sums(): pl.pallas_call(product, out_shape=jax.ShapeDtypeStruct((YL, NX, YH, BLOCK...  2.93 us
    ppermute x1, starting transfers between devices, per_device(): other = lax.ppermute(own, 'c', [(0, 1), (1, 0)])  2.93 us
  transfers between devices with their start and end apart: 1, of which 1 were waited for; matrix products, arithmetic and copies ran while one was open for 0% of the time, Pallas kernels for 2%

profile of v11, /device:TPU:1, one launch (start us, length us, event | category | flops | bytes accessed | tf_op | source)
XLA Modules:
  0.0 100.2 jit_solution(13174326604159538088)
XLA Ops:
  0.0 0.0 copy-start
  0.0 0.9 copy-done
  0.9 0.1 shard_map.46
  1.0 0.0 copy-start.2
  1.0 0.0 copy-start.1
  1.0 46.4 %all-gather = f32[80,24,128]{2,1,0:T(8,128)S(1)} all-gather(f32[5,24,128]{2,1,0:T(8,128)S(1)} %shard_map.46), channel_id=2, replica_groups={{0,3,4,7,8,11,12,15,16,19,20,23,24,27,28,31},{30,29,26,25,22,21,18,17,1..., dimensions={0}, use_global_device_ids=true | all-gather | bytes 1044480 | tf_op jit(solution)/shard_map/all_gather | solution.py:159
  47.5 2.9 %collective-permute-start = (f32[16,5,24,128]{3,2,1,0:T(8,128)S(1)}, f32[16,5,24,128]{3,2,1,0:T(8,128)S(1)}, u32[]{:S(2)}, u32[]{:S(2)}) collective-permute-start(f32[16,5,24,128]{3,2,1,0:T(8,128)S(1)} %bitcast.5), channel_id=1, source_target_pairs={{0,1},{1,0},{2,3},{3,2},{4,5},{5,4},{6,7},{7,6},{8,9},{9,8},{10,11... | collective-permute-start | bytes 2949128 | tf_op jit(solution)/shard_map/ppermute | solution.py:160
  50.4 1.9 %shard_map.47 = (bf16[5,512,384]{2,1,0:T(8,128)(2,1)S(1)}, bf16[5,512,384]{2,1,0:T(8,128)(2,1)S(1)}) custom-call(f32[5,384,384]{2,1,0:T(8,128)} %integrals_ref.1), custom_call_target="tpu_custom_call" | custom-call | flops 5000000 | bytes 7000000 | tf_op jit(solution)/shard_map/pallas_call | solution.py:42
  52.3 0.0 copy-done.2
  52.4 0.0 copy-done.1
  52.4 0.1 pad_add_fusion.meta_ref
  52.5 0.1 collective-permute-done.other_ref
  52.6 2.9 %shard_map.48 = f32[2,4,4,5,8,384]{5,4,3,2,1,0:T(8,128)S(1)} custom-call(s32[16]{0:T(128)S(1)} %pad_add_fusion.meta_ref, f32[16,5,24,128]{3,2,1,0:T(8,128)S(1)} %bitcast.6, f32[16,5,24,128]{3,2,1,0:T(8,128)S(1)} %collective-permute-done.other_ref, bf16[5,512,384]{2,1,0:T(8,128)(2,1)S(1)} %get-tuple-element.7.bhi_ref, ...), custom_call_target="tpu_custom_call" | custom-call | flops 1200000000 | bytes 8000000 | tf_op jit(solution)/shard_map/pallas_call | solution.py:116
  55.5 29.4 %all_to_all.10 = f32[8,160,384]{2,1,0:T(8,128)S(1)} all-to-all(f32[8,160,384]{2,1,0:T(8,128)S(1)} %bitcast.4), channel_id=1, replica_groups=mesh['yh'=4,'yl'=2,'x'=4,'zh'=4,'zl'=4,'c'=2] {'yl','x'}, dimensions={0} | all-to-all | bytes 3932160 | tf_op jit(solution)/shard_map/all_to_all | solution.py:163
  84.9 0.1 reduce_sum.9
  85.0 13.9 %all_to_all.11.parts_ref = f32[4,40,384]{2,1,0:T(8,128)S(1)} all-to-all(f32[4,40,384]{2,1,0:T(8,128)S(1)} %bitcast.7), channel_id=1, replica_groups=mesh['yh'=4,'yl'=2,'x'=4,'zh'=4,'zl'=4,'c'=2] {'yh'}, dimensions={0} | all-to-all | bytes 491520 | tf_op jit(solution)/shard_map/all_to_all | solution.py:164
  99.0 1.2 %shard_map.49 = f32[5,8,384]{2,1,0:T(8,128)} custom-call(s32[16]{0:T(128)S(1)} %pad_add_fusion.meta_ref, f32[4,40,384]{2,1,0:T(8,128)S(1)} %all_to_all.11.parts_ref), custom_call_target="tpu_custom_call" | custom-call | tf_op jit(solution)/shard_map/pallas_call | solution.py:139
  (2 shorter events, 0.0 us)
Async XLA Ops:
  0.0 0.9 copy-start
  1.0 51.3 %copy-start.2 = (s32[5]{0:T(128)S(1)}, s32[5]{0:T(128)}, u32[]{:S(2)}) copy-start(s32[5]{0:T(128)} %param.7) | copy-start | bytes 64
  1.0 51.3 %copy-start.1 = (s32[5]{0:T(128)S(1)}, s32[5]{0:T(128)}, u32[]{:S(2)}) copy-start(s32[5]{0:T(128)} %param.6) | copy-start | bytes 64
  47.5 5.1 %collective-permute-start = (f32[16,5,24,128]{3,2,1,0:T(8,128)S(1)}, f32[16,5,24,128]{3,2,1,0:T(8,128)S(1)}, u32[]{:S(2)}, u32[]{:S(2)}) collective-permute-start(f32[16,5,24,128]{3,2,1,0:T(8,128)S(1)} %bitcast.5), channel_id=1, source_target_pairs={{0,1},{1,0},{2,3},{3,2},{4,5},{5,4},{6,7},{7,6},{8,9},{9,8},{10,11... | collective-permute-start | bytes 2949128 | tf_op jit(solution)/shard_map/ppermute | solution.py:160
